TPU v7x, 32 devices: a whole 2x2x4 slice. The times are simulated.
32 devices in a mesh: group: 8 (over y, x, core), mp: 4 (over z).
Axes of the slice: x: 2, y: 2, z: 4, core: 2. Of those that a mesh axis runs over, the one named last changes fastest.
Arguments:
- hidden: bfloat16 [4096, 1792], P('group')
- norm_gain: float32 [1792], replicated, may hold values from 0.1 to 1.9
- qkv_weight: bfloat16 [1792, 2304], P(None, 'mp'), may hold values from -0.125 to 0.125
- out_weight: bfloat16 [1792, 1792], P('mp'), may hold values from -0.125 to 0.125
- adapter_down: bfloat16 [1792, 512], P(None, 'mp'), may hold values from -0.125 to 0.125
- adapter_up: bfloat16 [512, 1792], P('mp'), may hold values from -1.5 to 1.5
- vocab_rows: bfloat16 [512, 1792], P(('group', 'mp')), may hold values from -0.125 to 0.125
- segments: int32 [4096], P('group'), may hold values from 0 to 31, never falling along the last dimension, each value on 1 to 512 neighbouring positions
- request_adapter: int32 [32], replicated, may hold values from 0 to 31
- adapter_slot: int32 [32], replicated, may hold values from 0 to 31, each once
- page_table: int32 [128], replicated, may hold values from 0 to 127, as said below
Outputs:
- layer_update: bfloat16 [4096, 1792], P('group', 'mp')
- state_norms: float32 [16, 4096], P('mp', 'group')
- max_logits: float32 [4096], P(('group', 'mp'))
Inputs may be any that keep to these rules, and one draw needn't show every extreme that they name: A permutation of all pages. Logical page k of group g (entry g * 16 + k) lies in group page_table[g * 16 + k] // 16, and every group holds exactly two of the logical pages of every group. `segments`: every request's tokens stand together and in order; no request has more than 512 tokens. `adapter_slot`: A permutation.
All inputs are finite; a program needn't handle non-finite values.
Results may differ from a plain program's by a relative error of at most 0.013.
Values may be sent and summed in bfloat16 or wider, within the bound.
No kernel may reach another device: no remote copies, remote signals or barrier semaphores. Data moves between devices by JAX's collectives and lax.ppermute only.
A program may use at most 64 MiB of HBM per device.

v0:
```python
import functools

import jax
import jax.numpy as jnp
import numpy as np
from jax import lax
from jax.experimental import pallas as pl
from jax.experimental.pallas import tpu as pltpu
from jax.sharding import PartitionSpec as P

FEAT = 16
HD = 112
RANK = 16
EPSILON = 1e-05
HEAD = 2 * FEAT + HD
PHI = 1 + FEAT + FEAT * (FEAT + 1) // 2
PHI_PAD = 160
LANES = 128
ONE, TAG, REST = HD, HD + 1, HD + 2
NEAR = (0, 1, -1)
MIB = 1024 * 1024
VMEM_LIMIT = 60 * MIB

BF = jnp.bfloat16
F32 = jnp.float32
SMEM = pl.BlockSpec(memory_space=pltpu.SMEM)
VMEM = pl.BlockSpec(memory_space=pltpu.VMEM)
ANY = pl.BlockSpec(memory_space=pltpu.HBM)


def feature_tables():
    left = np.zeros((PHI_PAD, FEAT), np.float32)
    right = np.zeros((PHI_PAD, FEAT), np.float32)
    cols = np.zeros((PHI_PAD, 8), np.float32)
    cols[0, :3] = 1.0
    at = 1
    for i in range(FEAT):
        left[at, i] = 1.0
        cols[at, 1] = 1.0
        cols[at, 2] = FEAT**-0.25
        at += 1
    for i in range(FEAT):
        for j in range(i, FEAT):
            left[at, i] = 1.0
            right[at, j] = 1.0
            cols[at, 2] = (1.0 if i == j else 2.0**0.5) / (2.0 * FEAT) ** 0.5
            at += 1
    return left.astype(jnp.bfloat16), right.astype(jnp.bfloat16), cols


def dot(a, b, dims=((1,), (0,))):
    return lax.dot_general(a, b, (dims, ((), ())), preferred_element_type=F32)


def kernel_call(body, out_shape, in_specs, out_specs, scratch, flops, nbytes, limit=VMEM_LIMIT, aliases=None):
    return pl.pallas_call(
        body,
        out_shape=out_shape,
        in_specs=in_specs,
        out_specs=out_specs,
        scratch_shapes=scratch,
        input_output_aliases=aliases or {},
        compiler_params=pltpu.CompilerParams(vmem_limit_bytes=limit),
        cost_estimate=pl.CostEstimate(flops=flops, bytes_accessed=nbytes, transcendentals=0),
    )


def start(source, target, sem):
    copy = pltpu.make_async_copy(source, target, sem)
    copy.start()
    return copy


def packing(rows, columns):
    tiles, rest = divmod(columns, LANES)
    share = LANES // rest if rest and LANES % rest == 0 else 1
    if rows % (16 * share):
        share = 1
    return tiles, rest, share, tiles * rows + (rows // share if rest else 0)


def pack(block, target, base):
    rows = block.shape[0]
    tiles, rest, share, _ = packing(*block.shape)
    for t in range(tiles):
        target[base + t * rows : base + (t + 1) * rows, :] = block[:, t * LANES : (t + 1) * LANES].astype(BF)
    if rest:
        short = rows // share
        last = [block[q * short : (q + 1) * short, tiles * LANES :] for q in range(share)]
        if share * rest < LANES:
            last.append(jnp.zeros((short, LANES - share * rest), block.dtype))
        at = base + tiles * rows
        target[at : at + short, :] = jnp.concatenate(last, axis=1).astype(BF)


def unpack(source, base, target, row, rows, columns):
    tiles, rest, share, _ = packing(rows, columns)
    for t in range(tiles):
        piece = source[base + t * rows : base + (t + 1) * rows, :]
        target[row : row + rows, t * LANES : (t + 1) * LANES] = piece.astype(target.dtype)
    if rest:
        short = rows // share
        at = base + tiles * rows
        last = source[at : at + short, :].astype(F32)
        for q in range(share):
            piece = last[:, q * rest : (q + 1) * rest].astype(target.dtype)
            target[row + q * short : row + (q + 1) * short, tiles * LANES : columns] = piece


def staged_call(body, out_shape, scalars, operands, scratch, flops, nbytes, given=(), limit=VMEM_LIMIT):
    buffers = [pltpu.VMEM(x.shape, x.dtype) for x in list(operands) + list(out_shape)]
    ins, outs = len(operands), len(out_shape)

    def run(*refs):
        values, refs = refs[: len(scalars)], refs[len(scalars) :]
        ready, refs = refs[: len(given)], refs[len(given) :]
        far, refs = refs[: ins + outs], refs[ins + outs :]
        near, extra, sems = refs[: ins + outs], refs[ins + outs : -1], refs[-1]
        loads = [start(far[k], near[k], sems.at[k]) for k in range(ins)]
        for load in loads:
            load.wait()
        body(*values, *ready, *near, *extra)
        sends = [start(near[k], far[k], sems.at[k]) for k in range(ins, ins + outs)]
        for send in sends:
            send.wait()

    return kernel_call(
        run,
        [pltpu.HBM(x.shape, x.dtype) for x in out_shape],
        [SMEM] * len(scalars) + [VMEM] * len(given) + [ANY] * ins,
        [ANY] * outs,
        buffers + list(scratch) + [pltpu.SemaphoreType.DMA((ins + outs,))],
        flops,
        nbytes,
        limit,
    )(*scalars, *given, *operands)


def pick_pages(table, own, picked, groups, per_group, per_peer):
    def one_group(g, carry):
        spot = g * per_peer
        for k in range(per_group):
            local = table[g * per_group + k] - own * per_group
            picked[spot] = local
            spot = spot + jnp.where((local >= 0) & (local < per_group), 1, 0)
        return carry

    lax.fori_loop(0, groups, one_group, 0)


def place_pages(table, own, seen, source, target, groups, per_group, per_peer, page_len):
    for g in range(groups):
        seen[g] = 0
    for k in range(per_group):
        holder = lax.div(table[own * per_group + k], per_group)
        slot = holder * per_peer + seen[holder]
        seen[holder] = seen[holder] + 1
        start = pl.multiple_of(slot * page_len, page_len)
        target[k * page_len : (k + 1) * page_len, :] = source[pl.ds(start, page_len), :]


def picked_rows(source, picked, g, per_peer, page_len):
    pages = []
    for b in range(per_peer):
        at = pl.multiple_of(picked[g * per_peer + b] * page_len, page_len)
        pages.append(source[pl.ds(at, page_len), :])
    return jnp.concatenate(pages, axis=0)


def project_kernel(
    dims, table, hidden_in, gain, wq_in, wd_in, out_in, hidden, wq, wd, normed, wide, out, picked, sems
):
    groups, per_group, per_peer, page_len = dims
    rows, model_width = hidden.shape
    low = wd.shape[1]
    pieces = 4
    part = rows // pieces
    strip = wq.shape[0] // 2
    loads = [
        start(hidden_in.at[pl.ds(k * part, part)], hidden.at[pl.ds(k * part, part)], sems.at[k]) for k in range(pieces)
    ]
    weights = [start(wd_in, wd, sems.at[pieces])]
    for k in range(2):
        half = pl.ds(k * strip, strip)
        weights.append(start(wq_in.at[half], wq.at[half], sems.at[pieces + 1 + k]))
    pick_pages(table, lax.axis_index("group"), picked, groups, per_group, per_peer)
    step = 32
    scale = gain[...].reshape(1, model_width)

    def norm_rows(i, carry):
        at = pl.ds(pl.multiple_of(i * step, step), step)
        x = hidden[at, :].astype(F32)
        meansq = jnp.mean(x * x, axis=-1, keepdims=True)
        normed[at, :] = (x * lax.rsqrt(meansq + EPSILON) * scale).astype(BF)
        return carry

    for k in range(pieces):
        loads[k].wait()
        lax.fori_loop(k * part // step, (k + 1) * part // step, norm_rows, 0, unroll=2)
    for load in weights:
        load.wait()
    wide[:, :low] = dot(normed[...], wd[...])
    wide[:, low:] = dot(normed[...], wq[...], ((1,), (1,)))
    sends = []
    for g in range(groups):
        pack(picked_rows(wide, picked, g, per_peer, page_len), out.at[g], 0)
        sends.append(start(out.at[g], out_in.at[g], sems.at[pieces + 3 + g]))
    for send in sends:
        send.wait()


def residual_kernel(dims, shards, base, table, hidden_in, out_in, window, wide, pages, picked, sems):
    groups, per_group, per_peer, page_len = dims
    own_shard = lax.axis_index("mp")
    for j in range(shards):

        @pl.when(own_shard == j)
        def _(j=j):
            columns, _ = column_window(j, shards, hidden_in.shape[1])
            start(hidden_in.at[:, columns], window, sems.at[groups])

    pick_pages(table, lax.axis_index("group"), picked, groups, per_group, per_peer)
    pltpu.make_async_copy(hidden_in.at[:, 0 : window.shape[1]], window, sems.at[groups]).wait()
    for j in range(shards):

        @pl.when(own_shard == j)
        def _(j=j):
            _, at = column_window(j, shards, hidden_in.shape[1])
            wide[...] = window[:, at : at + wide.shape[1]].astype(F32)

    sends = []
    for g in range(groups):
        pack(picked_rows(wide, picked, g, per_peer, page_len), pages.at[g], 0)
        sends.append(start(pages.at[g], out_in.at[g, pl.ds(base, pages.shape[1])], sems.at[g]))
    for send in sends:
        send.wait()


def products_kernel(groups, shards, w_out_in, w_up_in, *refs):
    blocks = refs[:shards]
    _, out_in, vocab, w_out, w_up, products, shared, sems = refs[shards:]
    inner, model_width = w_out.shape
    low = w_up.shape[0]
    width = model_width // shards
    held = blocks[0].shape[0]
    loads = [start(w_up_in, w_up, sems.at[groups])]
    for k in range(inner // HD):
        rows = pl.ds(k * HD, HD)
        loads.append(start(w_out_in.at[rows], w_out.at[rows], sems.at[groups + 1 + k]))
    own_shard = lax.axis_index("mp")
    for i in range(shards):
        at = lax.rem(own_shard + i + 1, shards) * held
        vocab[pl.ds(pl.multiple_of(at, held), held), :] = blocks[i][...]
    for load in loads:
        load.wait()
    products[:, :inner] = dot(vocab[...], w_out[...], ((1,), (1,)))
    products[:, inner : inner + low] = dot(vocab[...], w_up[...], ((1,), (1,)))
    for j in range(shards):

        @pl.when(own_shard == j)
        def _(j=j):
            products[:, inner + low :] = vocab[:, j * width : (j + 1) * width].astype(F32)

    pack(products[...], shared, 0)
    sends = [start(shared, out_in.at[g, pl.ds(0, shared.shape[0])], sems.at[g]) for g in range(groups)]
    for send in sends:
        send.wait()


def phi_of(vectors, left, right, cols):
    first = dot(left[...], vectors) + cols[:, 0:1]
    second = dot(right[...], vectors) + cols[:, 1:2]
    return first * second * cols[:, 2:3]


def with_ones(values):
    lane = lax.broadcasted_iota(jnp.int32, (values.shape[0], LANES - HD), 1)
    return jnp.concatenate([values, jnp.where(lane == 0, 1.0, 0.0).astype(values.dtype)], axis=1)


def with_ones_t(values):
    row = lax.broadcasted_iota(jnp.int32, (LANES - HD, values.shape[1]), 0)
    return jnp.concatenate([values, jnp.where(row == 0, 1.0, 0.0).astype(values.dtype)], axis=0)


def same_upto(segrow):
    count = segrow.shape[1]
    ids = segrow[...].astype(F32)
    column = jnp.transpose(jnp.broadcast_to(ids, (8, count)))[:, 0:1]
    behind = lax.broadcasted_iota(jnp.int32, (count, count), 0)
    ahead = lax.broadcasted_iota(jnp.int32, (count, count), 1)
    return jnp.where((column == ids) & (behind <= ahead), 1.0, 0.0)


def group_kernel(
    dims, low, heads, table, arrived, segrow, left, right, cols, ordered_in, ordered_t_in, state_in, nd_in,
    state, wide, placed, ordered, ordered_t, nd, mask, seen, sems
):
    groups, per_group, per_peer, page_len = dims
    tall = per_peer * page_len
    count, sent = placed.shape
    mask[...] = same_upto(segrow)
    for g in range(groups):
        unpack(arrived.at[g], 0, wide, g * tall, tall, sent)
    place_pages(table, lax.axis_index("group"), seen, wide, placed, groups, per_group, per_peer, page_len)
    ordered[...] = placed[:, low:].astype(BF)
    for at in range(0, sent, LANES):
        end = min(at + LANES, sent)
        ordered_t[at:end, :] = jnp.transpose(placed[:, at:end]).astype(BF)
    sends = [start(ordered_t, ordered_t_in, sems.at[0]), start(ordered, ordered_in, sems.at[1])]

    last = segrow[:, count - 1 : count]
    member = jnp.where(segrow[...] == last, 1.0, 0.0)
    total = jnp.sum(member, axis=1, keepdims=True)
    fine = total - total.astype(BF).astype(F32)
    tag = last.astype(F32) + 1.0
    row = lax.broadcasted_iota(jnp.int32, (PHI_PAD, LANES), 0)
    lane = lax.broadcasted_iota(jnp.int32, (PHI_PAD, LANES), 1)
    block = 256 if count % 256 == 0 else count
    for h in range(heads):
        at = h * HEAD
        key = ordered[:, at + FEAT : at + 2 * FEAT] * BF(0.25)
        value = ordered[:, at + 2 * FEAT : at + HEAD]
        at = low + h * HEAD
        query_t = ordered_t[at : at + FEAT, :]
        key_t = ordered_t[at + FEAT : at + 2 * FEAT, :]
        extended_t = with_ones_t(ordered_t[at + 2 * FEAT : at + HEAD, :])

        phi = (phi_of(key_t, left, right, cols) * member).astype(BF)
        summed = dot(phi, with_ones(value))
        summed = jnp.where((row == 0) & (lane == TAG), tag, summed)
        summed = jnp.where((row == 0) & (lane == REST), fine, summed)
        state[h] = summed.astype(BF)

        for begin in range(0, count, block):
            end = begin + block
            s = dot(key[:end], query_t[:, begin:end])
            w = (1.0 + s * (1.0 + 0.5 * s)) * mask[:end, begin:end]
            nd[h, :, begin:end] = dot(extended_t[:, :end], w.astype(BF))
        sends.append(start(nd.at[h], nd_in.at[h], sems.at[3 + h]))
    sends.append(start(state, state_in, sems.at[2]))
    for send in sends:
        send.wait()


def split3(x):
    a = x.astype(BF)
    rest = x - a.astype(F32)
    b = rest.astype(BF)
    return jnp.concatenate([a, b, (rest - b.astype(F32)).astype(BF)], axis=0)


def state_corner(state):
    corner = state[0, 0:1, :].astype(F32)
    return corner[:, TAG : TAG + 1], corner[:, ONE : ONE + 1] + corner[:, REST : REST + 1]


def column_window(j, shards, model_width):
    width = model_width // shards
    size = window_size(shards, model_width)
    first = min(j * width // LANES * LANES, model_width - size)
    return slice(first, first + size), j * width - first


def window_size(shards, model_width):
    width = model_width // shards
    return max(-(-(j * width % LANES + width) // LANES) * LANES for j in range(shards))


def each_shard(offsets, shards):
    for k, offset in enumerate(offsets):
        for own in range(shards):
            if 0 <= own + offset < shards:
                yield k, own, own + offset


def shard_parts(offsets, shards, w_out_in, w_up_in, weights, w_sems, inputs, held_out, outs, sems):
    own_shard = lax.axis_index("mp")
    inner, model_width = w_out_in.shape
    width = model_width // shards

    def copies(k, j):
        window, _ = column_window(j, shards, model_width)
        return (
            pltpu.make_async_copy(w_out_in.at[:, window], weights.at[k, pl.ds(0, inner)], w_sems.at[2 * k]),
            pltpu.make_async_copy(
                w_up_in.at[:, window], weights.at[k, pl.ds(inner, w_up_in.shape[0])], w_sems.at[2 * k + 1]
            ),
        )

    def fetch():
        for k, own, j in each_shard(offsets, shards):

            @pl.when(own_shard == own)
            def _(k=k, j=j):
                for copy in copies(k, j):
                    copy.start()

    def compute():
        for k, own, j in each_shard(offsets, shards):

            @pl.when(own_shard == own)
            def _(k=k, j=j):
                for copy in copies(k, j):
                    copy.wait()
                _, at = column_window(j, shards, model_width)
                held_out[k] = dot(weights[k, :, at : at + width], inputs[...], ((0,), (0,))).astype(BF)
                start(held_out.at[k], outs[k], sems.at[k])

    def finish():
        for k, own, j in each_shard(offsets, shards):

            @pl.when(own_shard == own)
            def _(k=k):
                pltpu.make_async_copy(held_out.at[k], outs[k], sems.at[k]).wait()

    return fetch, compute, finish


def finish_kernel(
    low, heads, shards, ordered_t_in, nd_in, state, segrow, slotrow, left, right, cols, w_out_in, w_up_in, *refs
):
    far = far_offsets(shards)
    outs = refs[: len(far) - 1]
    outs = [outs[0], *outs]
    inputs_in, queries, nd, weights, inputs, held_out, sems, w_sems = refs[len(far) - 1 :]
    inner = heads * HD
    sem = iter(range(len(far), len(far) + 2 * heads + 2))
    lows = start(ordered_t_in.at[pl.ds(0, low)], inputs.at[pl.ds(inner, low)], sems.at[next(sem)])
    fetches = []
    for h in range(heads):
        rows = pl.ds(low + h * HEAD, FEAT)
        fetches.append(start(ordered_t_in.at[rows], queries.at[h], sems.at[next(sem)]))
        fetches.append(start(nd_in.at[h], nd.at[h], sems.at[next(sem)]))
    fetch_weights, compute, finish = shard_parts(
        far, shards, w_out_in, w_up_in, weights, w_sems, inputs, held_out, outs, sems
    )
    fetch_weights()
    tag, _ = state_corner(state)
    carried = jnp.where(segrow[...].astype(F32) + 1.0 == tag, 1.0, 0.0)
    row_slot = lax.div(lax.broadcasted_iota(jnp.int32, (low, 1), 0), RANK)
    lows.wait()
    lowered = jnp.where(slotrow[...] == row_slot, inputs[inner:, :].astype(F32), 0.0)
    inputs[inner:, :] = lowered.astype(BF)
    for h in range(heads):
        fetches[2 * h].wait()
        fetches[2 * h + 1].wait()
        cross = dot(state[h], phi_of(queries[h], left, right, cols).astype(BF), ((0,), (0,)))
        both = nd[h] + carried * cross
        inputs[h * HD : (h + 1) * HD, :] = (both[:HD, :] / both[ONE : ONE + 1, :]).astype(BF)
    compute()
    kept = start(inputs, inputs_in, sems.at[next(sem)])
    finish()
    kept.wait()


def far_offsets(shards):
    far = [shards - 1, 1 - shards]
    for distance in range(shards - 2, 1, -1):
        far += [distance, -distance]
    return far


def near_kernel(shards, w_out_in, w_up_in, inputs_in, *refs):
    outs = refs[: len(NEAR)]
    weights, inputs, held_out, sems, w_sems = refs[len(NEAR) :]
    load = start(inputs_in, inputs, sems.at[len(NEAR)])
    fetch, compute, finish = shard_parts(NEAR, shards, w_out_in, w_up_in, weights, w_sems, inputs, held_out, outs, sems)
    fetch()
    load.wait()
    compute()
    finish()


def logits_kernel(dims, shards, width, table, arrived, inputs, out, vocab, both, wide, placed, seen):
    groups, per_group, per_peer, page_len = dims
    tall = per_peer * page_len
    inner = inputs.shape[0]
    rows = vocab.shape[0] // groups
    _, _, _, base = packing(rows, inner + width)
    for g in range(groups):
        unpack(arrived.at[g], 0, vocab, g * rows, rows, inner + width)
        unpack(arrived.at[g], base, wide, g * tall, tall, width)
    place_pages(table, lax.axis_index("group"), seen, wide, placed, groups, per_group, per_peer, page_len)
    both[:inner, :] = inputs[...]
    both[inner:, :] = jnp.transpose(placed[...]).astype(BF)
    block = inputs.shape[1] // shards
    scored = dot(vocab[...], both[...])
    for j in range(shards):
        out[j] = scored[:, j * block : (j + 1) * block].astype(BF)


def norms_kernel(low, heads, ordered, ordered_t, state, segrow, left, right, cols, norms, mask):
    count = segrow.shape[1]
    mask[...] = same_upto(segrow)
    upto = mask[...].astype(BF)
    tag, held = state_corner(state)
    carried = jnp.where(segrow[...].astype(F32) + 1.0 == tag, 1.0, 0.0)
    value_lane = lax.broadcasted_iota(jnp.int32, (1, LANES), 1) < HD
    counted = carried * held + jnp.sum(mask[...], axis=0, keepdims=True)
    block = 256 if count % 256 == 0 else count
    increments = []
    before = []
    for h in range(heads):
        at = h * HEAD
        key = ordered[:, at + FEAT : at + 2 * FEAT] * BF(0.25)
        value = ordered[:, at + 2 * FEAT : at + HEAD]
        at = low + h * HEAD
        key_t = ordered_t[at + FEAT : at + 2 * FEAT, :]
        value_t = ordered_t[at + 2 * FEAT : at + HEAD, :]
        wide_key = key_t.astype(F32)
        wide_value = value_t.astype(F32)
        self_score = 0.25 * jnp.sum(wide_key * wide_key, axis=0, keepdims=True)
        self_value = jnp.sum(wide_value * wide_value, axis=0, keepdims=True)
        diagonal = (1.0 + self_score * (1.0 + 0.5 * self_score)) * self_value
        below = []
        for begin in range(0, count, block):
            end = begin + block
            kk = dot(key[:end], key_t[:, begin:end])
            vv = dot(value[:end], value_t[:, begin:end])
            gram = (1.0 + kk * (1.0 + 0.5 * kk)) * vv * mask[:end, begin:end]
            below.append(jnp.sum(gram, axis=0, keepdims=True))
        added = 2.0 * jnp.concatenate(below, axis=1) - diagonal
        held_state = state[h]
        against = dot(held_state, phi_of(key_t, left, right, cols).astype(BF), ((0,), (0,)))[:HD, :]
        along = jnp.sum(against * wide_value, axis=0, keepdims=True)
        increments.append(added + 2.0 * carried * along)
        wide_state = jnp.where(value_lane, held_state.astype(F32), 0.0)
        per_lane = jnp.sum(wide_state * wide_state, axis=0, keepdims=True)
        before.append(jnp.sum(per_lane, axis=1, keepdims=True))
    if heads % 8:
        increments.append(jnp.zeros((8 - heads % 8, count), F32))
    stacked = split3(jnp.concatenate(increments, axis=0))
    thrice = dot(stacked, upto)
    rows = thrice.shape[0] // 3
    summed = thrice[:rows] + thrice[rows : 2 * rows] + thrice[2 * rows :]
    for h in range(heads):
        total = carried * before[h] + summed[h : h + 1, :]
        norms[h : h + 1, :] = jnp.sqrt(total / (counted * float(FEAT * HD)))


def best_kernel(shards, pieces, best):
    whole = pieces[0].astype(F32)
    for i in range(1, shards):
        whole = whole + pieces[i].astype(F32)
    best[...] = jnp.max(whole, axis=0, keepdims=True)


def exchange(blocks, axis):
    return lax.all_to_all(blocks, axis, split_axis=0, concat_axis=0, tiled=True)


def ring_rows(values, axis):
    size = lax.axis_size(axis)
    steps = [lax.ppermute(values, axis, [(i, (i + by) % size) for i in range(size)]) for by in range(size - 1, 0, -1)]
    return [*steps, values]


def line_sums(terms, axis, beside):
    size = lax.axis_size(axis)

    def joined(*parts):
        return sum(part.astype(F32) for part in parts).astype(BF)

    def up(values, first, last):
        return lax.ppermute(values, axis, [(i, i + 1) for i in range(first, last)])

    def down(values, first, last):
        return lax.ppermute(values, axis, [(i, i - 1) for i in range(first, last)])

    if size == 4:
        relayed_up = up(terms[2], 0, size - 2)
        relayed_down = down(terms[-2], 2, size)
        far = lax.ppermute(terms[3], axis, [(0, 3), (3, 0)])
        relayed_up, relayed_down, far, beside = lax.optimization_barrier((relayed_up, relayed_down, far, beside))
        near_up = up(joined(terms[1], relayed_up), 0, size - 1)
        near_down = down(joined(terms[-1], relayed_down), 1, size)
        return joined(terms[0], far, near_up, near_down), beside
    going_up = going_down = None
    for step in range(1, size):
        to_up = terms[size - step]
        to_down = terms[step - size]
        if step > 1:
            to_up = joined(to_up, going_up)
            to_down = joined(to_down, going_down)
        going_up = up(to_up, 0, step)
        going_down = down(to_down, size - step, size)
    return joined(terms[0], going_up, going_down), beside


def on_device(
    hidden,
    norm_gain,
    qkv_weight,
    out_weight,
    adapter_down,
    adapter_up,
    vocab_rows,
    segments,
    request_adapter,
    adapter_slot,
    page_table,
):
    groups = lax.axis_size("group")
    shards = lax.axis_size("mp")
    own_shard = lax.axis_index("mp")
    count, model_width = hidden.shape
    per_group = page_table.shape[0] // groups
    per_peer = per_group // groups
    page_len = count // per_group
    dims = (groups, per_group, per_peer, page_len)
    qkv_cols = qkv_weight.shape[1]
    heads = qkv_cols // HEAD
    low = adapter_down.shape[1]
    inner = heads * HD
    width = model_width // shards
    sent = low + qkv_cols
    tall = per_peer * page_len
    packed = packing(tall, sent)[-1]
    some = shards * vocab_rows.shape[0]
    scored = groups * some
    aside = packing(some, inner + low + width)[-1] + packing(tall, width)[-1]
    shape = jax.ShapeDtypeStruct
    dma = pltpu.SemaphoreType.DMA
    picked = pltpu.SMEM((groups * per_peer + 1,), jnp.int32)

    left, right, cols = [jnp.asarray(t) for t in feature_tables()]
    segrow = segments.reshape(1, count)
    request_ids = jnp.arange(request_adapter.shape[0], dtype=jnp.int32)
    adapter_ids = jnp.arange(adapter_slot.shape[0], dtype=jnp.int32)

    outgoing = kernel_call(
        functools.partial(project_kernel, dims),
        pltpu.HBM((groups, packed, LANES), BF),
        [SMEM, ANY, VMEM, ANY, ANY],
        ANY,
        [
            pltpu.VMEM((count, model_width), BF),
            pltpu.VMEM((qkv_cols, model_width), BF),
            pltpu.VMEM((model_width, low), BF),
            pltpu.VMEM((count, model_width), BF),
            pltpu.VMEM((count, sent), F32),
            pltpu.VMEM((groups, packed, LANES), BF),
            picked,
            dma((7 + groups,)),
        ],
        2 * count * model_width * sent,
        2 * (count * model_width + model_width * sent),
    )(page_table, hidden, norm_gain, qkv_weight.T, adapter_down)
    arrived = exchange(outgoing, "group")

    after_vocab, after_adapter, later_hidden, _ = lax.optimization_barrier(
        (vocab_rows, request_adapter, hidden, outgoing)
    )
    some_vocab = ring_rows(after_vocab, "mp")
    request_slot = jnp.sum(jnp.where(after_adapter[:, None] == adapter_ids[None, :], adapter_slot[None, :], 0), axis=1)
    slots = jnp.sum(jnp.where(segrow == request_ids[:, None], request_slot[:, None], 0), axis=0, keepdims=True)
    slotrow = slots - own_shard * (low // RANK)
    window = window_size(shards, model_width)
    ahead = packing(some, inner + low + width)[-1]
    beside = kernel_call(
        functools.partial(residual_kernel, dims, shards, ahead),
        pltpu.HBM((groups, aside, LANES), BF),
        [SMEM, ANY],
        ANY,
        [
            pltpu.VMEM((count, window), BF),
            pltpu.VMEM((count, width), F32),
            pltpu.VMEM((groups, packing(tall, width)[-1], LANES), BF),
            picked,
            dma((groups + 1,)),
        ],
        1,
        1,
    )(page_table, later_hidden)
    beside = kernel_call(
        functools.partial(products_kernel, groups, shards),
        pltpu.HBM((groups, aside, LANES), BF),
        [ANY, ANY] + [VMEM] * shards + [ANY],
        ANY,
        [
            pltpu.VMEM((some, model_width), BF),
            pltpu.VMEM((inner, model_width), BF),
            pltpu.VMEM((low, model_width), BF),
            pltpu.VMEM((some, inner + low + width), F32),
            pltpu.VMEM((ahead, LANES), BF),
            dma((groups + 1 + heads,)),
        ],
        2 * some * model_width * (inner + low),
        2 * count * model_width,
        44 * MIB,
        {2 + shards: 0},
    )(out_weight, adapter_up, *some_vocab, beside)
    arrived, beside, slotrow = lax.optimization_barrier((arrived, beside, slotrow))

    ordered, ordered_t, state, nd = kernel_call(
        functools.partial(group_kernel, dims, low, heads),
        (
            pltpu.HBM((count, qkv_cols), BF),
            pltpu.HBM((sent, count), BF),
            pltpu.HBM((heads, PHI_PAD, LANES), BF),
            pltpu.HBM((heads, LANES, count), F32),
        ),
        [SMEM] + [VMEM] * 5,
        (ANY, ANY, ANY, ANY),
        [
            pltpu.VMEM((heads, PHI_PAD, LANES), BF),
            pltpu.VMEM((count, sent), F32),
            pltpu.VMEM((count, sent), F32),
            pltpu.VMEM((count, qkv_cols), BF),
            pltpu.VMEM((sent, count), BF),
            pltpu.VMEM((heads, LANES, count), F32),
            pltpu.VMEM((count, count), F32),
            pltpu.SMEM((groups,), jnp.int32),
            dma((3 + heads,)),
        ],
        heads * 2 * count * count * 512,
        6 * count * sent,
        40 * MIB,
    )(page_table, arrived, segrow, left, right, cols)
    beside, state = lax.optimization_barrier((beside, state))
    beside = exchange(beside, "group")
    state = lax.ppermute(state, "group", [(i, i + 1) for i in range(groups - 1)])

    far = far_offsets(shards)
    part = pltpu.HBM((width, count), BF)
    *far_terms, inputs = kernel_call(
        functools.partial(finish_kernel, low, heads, shards),
        [part] * (len(far) - 1) + [pltpu.HBM((inner + low, count), BF)],
        [ANY] * 2 + [VMEM] * 6 + [ANY] * 2,
        [ANY] * len(far),
        [
            pltpu.VMEM((heads, FEAT, count), BF),
            pltpu.VMEM((heads, LANES, count), F32),
            pltpu.VMEM((len(far), inner + low, window), BF),
            pltpu.VMEM((inner + low, count), BF),
            pltpu.VMEM((len(far), width, count), BF),
            dma((len(far) + 2 * heads + 2,)),
            dma((2 * len(far),)),
        ],
        20 * count * (inner + low) * model_width,
        40 * count * model_width,
    )(ordered_t, nd, state, segrow, slotrow, left, right, cols, out_weight, adapter_up)
    near_terms = kernel_call(
        functools.partial(near_kernel, shards),
        [part] * len(NEAR),
        [ANY] * 3,
        [ANY] * len(NEAR),
        [
            pltpu.VMEM((len(NEAR), inner + low, window), BF),
            pltpu.VMEM((inner + low, count), BF),
            pltpu.VMEM((len(NEAR), width, count), BF),
            dma((len(NEAR) + 1,)),
            dma((2 * len(NEAR),)),
        ],
        1,
        1,
    )(out_weight, adapter_up, inputs)
    terms = dict(zip(NEAR, near_terms)) | dict(zip(far, [far_terms[0], *far_terms]))
    [logits] = staged_call(
        functools.partial(logits_kernel, dims, shards, width),
        [shape((shards, scored, count // shards), BF)],
        [page_table],
        [inputs],
        [
            pltpu.VMEM((scored, inner + low + width), BF),
            pltpu.VMEM((inner + low + width, count), BF),
            pltpu.VMEM((count, width), F32),
            pltpu.VMEM((count, width), F32),
            pltpu.SMEM((groups,), jnp.int32),
        ],
        1,
        1,
        given=[beside],
        limit=(40 if scored <= 512 else 56) * MIB,
    )
    [state_norms] = staged_call(
        functools.partial(norms_kernel, low, heads),
        [shape((heads, count), F32)],
        [],
        [ordered, ordered_t, state, segrow, left, right, cols],
        [pltpu.VMEM((count, count), F32)],
        1,
        1,
    )
    update, [state_norms, _] = line_sums(terms, "mp", [state_norms, logits])
    logits = exchange(logits, "mp")
    best = kernel_call(
        functools.partial(best_kernel, shards),
        shape((1, count // shards), F32),
        [VMEM],
        VMEM,
        [],
        1,
        1,
        32 * MIB,
    )(logits)
    return update.T, state_norms, best.reshape(-1)


def solution(mesh):
    placed = (
        P("group", None),
        P(),
        P(None, "mp"),
        P("mp", None),
        P(None, "mp"),
        P("mp", None),
        P(("group", "mp"), None),
        P("group"),
        P(),
        P(),
        P(),
    )
    return jax.shard_map(
        on_device,
        mesh=mesh,
        in_specs=placed,
        out_specs=(P("group", "mp"), P("mp", "group"), P(("group", "mp"))),
        check_vma=False,
    )
```

profile of v0, /device:TPU:0, one launch (start us, length us, event | category | flops | bytes accessed | tf_op | source)
XLA Modules:
  0.0 92.1 jit_solution(16292362929022946997)
XLA Ops:
  0.7 6.2 %shard_map.157 = bf16[8,352,128]{2,1,0:T(8,128)(2,1)} custom-call(s32[128]{0:T(128)} %refs_0_.1, bf16[512,1792]{1,0:T(8,128)(2,1)} %hidden_in.2, f32[1792]{0:T(1024)} %gain.1, bf16[576,1792]{1,0:T(8,128)(2,1)} %bitcast.9, bf16[1792,128]{1,0:T(8,128)(2,1)} %wd_in.1), custom_call_target="tpu_custom_call" | custom-call | flops 1291845632 | bytes 4358144 | tf_op jit(solution)/shard_map/pallas_call | solution.py:632
  6.9 5.2 %all-to-all-start = ((bf16[8,352,128]{2,1,0:T(8,128)(2,1)}), bf16[8,352,128]{2,1,0:T(8,128)(2,1)S(1)}, u32[]{:S(2)}, u32[]{:S(2)}) async-start(bf16[8,352,128]{2,1,0:T(8,128)(2,1)} %shard_map.157), calls=%async_computation | async-start | bytes 1441792 | tf_op jit(solution)/shard_map/all_to_all | solution.py:550
  12.1 1.6 %collective-permute-start.2 = (bf16[16,1792]{1,0:T(8,128)(2,1)S(1)}, bf16[16,1792]{1,0:T(8,128)(2,1)S(1)}, u32[]{:S(2)}, u32[]{:S(2)}) collective-permute-start(bf16[16,1792]{1,0:T(8,128)(2,1)S(1)} %copy-done.4), channel_id=1, source_target_pairs={{0,1},{1,2},{2,3},{3,0},{4,5},{5,6},{6,7},{7,4},{8,9},{9,10},{10,1... | collective-permute-start | bytes 172040 | tf_op jit(solution)/shard_map/ppermute | solution.py:555
  13.7 2.6 %collective-permute-start.1 = (bf16[16,1792]{1,0:T(8,128)(2,1)S(1)}, bf16[16,1792]{1,0:T(8,128)(2,1)S(1)}, u32[]{:S(2)}, u32[]{:S(2)}) collective-permute-start(bf16[16,1792]{1,0:T(8,128)(2,1)S(1)} %copy-done.4), channel_id=1, source_target_pairs={{0,2},{1,3},{2,0},{3,1},{4,6},{5,7},{6,4},{7,5},{8,10},{9,11},{10,... | collective-permute-start | bytes 172040 | tf_op jit(solution)/shard_map/ppermute | solution.py:555
  16.3 1.4 %collective-permute-start = (bf16[16,1792]{1,0:T(8,128)(2,1)S(1)}, bf16[16,1792]{1,0:T(8,128)(2,1)S(1)}, u32[]{:S(2)}, u32[]{:S(2)}) collective-permute-start(bf16[16,1792]{1,0:T(8,128)(2,1)S(1)} %copy-done.4), channel_id=1, source_target_pairs={{0,3},{1,0},{2,1},{3,2},{4,7},{5,4},{6,5},{7,6},{8,11},{9,8},{10,9... | collective-permute-start | bytes 172040 | tf_op jit(solution)/shard_map/ppermute | solution.py:555
  17.6 0.2 select_reduce_fusion.1
  17.8 0.1 select_reduce_fusion
  17.9 0.6 broadcast_subtract_fusion
  18.5 2.9 %shard_map.158.refs_4_ = bf16[8,736,128]{2,1,0:T(8,128)(2,1)} custom-call(s32[128]{0:T(128)} %refs_0_.1, bf16[512,1792]{1,0:T(8,128)(2,1)} %hidden_in.2), custom_call_target="tpu_custom_call" | custom-call | flops 1 | bytes 1 | tf_op jit(solution)/shard_map/pallas_call | solution.py:661
  21.4 0.0 copy-start.3
  21.5 3.1 %shard_map.159 = bf16[8,736,128]{2,1,0:T(8,128)(2,1)} custom-call(bf16[448,1792]{1,0:T(8,128)(2,1)S(1)} %copy-done, bf16[128,1792]{1,0:T(8,128)(2,1)S(1)} %copy-done.2, bf16[16,1792]{1,0:T(8,128)(2,1)S(1)} %collective-permute-done.refs_0_, bf16[16,1792]{1,0:T(8,128)(2,1)S(1)} %collective-permute-done.1.refs_1_, ...), custom_call_target="tpu_custom_call", output_to_operand_aliasing={{}: (6, {})} | custom-call | flops 132120576 | bytes 1835008 | tf_op jit(solution)/shard_map/pallas_call | solution.py:676
  24.7 4.5 %shard_map.160 = (bf16[512,576]{1,0:T(8,128)(2,1)}, bf16[704,512]{1,0:T(8,128)(2,1)}, bf16[4,160,128]{2,1,0:T(8,128)(2,1)}, f32[4,128,512]{2,1,0:T(8,128)}) custom-call(s32[128]{0:T(128)S(1)} %copy-done.8, bf16[8,352,128]{2,1,0:T(8,128)(2,1)S(1)} %all-to-all-done.arrived, s32[1,512]{1,0:T(1,128)S(1)} %bitcast.8, bf16[160,16]{1,0:T(8,128)(2,1)S(1)} %copy-done.6, ...), custom_call_target="tpu_custom_call" | custom-call | flops 1073741824 | bytes 2162688 | tf_op jit(solution)/shard_map/pallas_call | solution.py:696
  29.2 1.5 %collective-permute-start.3 = (bf16[4,160,128]{2,1,0:T(8,128)(2,1)}, bf16[4,160,128]{2,1,0:T(8,128)(2,1)S(1)}, u32[]{:S(2)}, u32[]{:S(2)}) collective-permute-start(bf16[4,160,128]{2,1,0:T(8,128)(2,1)} %get-tuple-element.34), channel_id=1, source_target_pairs={{0,4},{4,8},{8,12},{12,16},{16,20},{20,24},{24,28},{1,5},{5,9},{9,... | collective-permute-start | bytes 491528 | tf_op jit(solution)/shard_map/ppermute | solution.py:723
  30.7 4.8 %all-to-all-start.1 = ((bf16[8,736,128]{2,1,0:T(8,128)(2,1)}), bf16[8,736,128]{2,1,0:T(8,128)(2,1)S(1)}, u32[]{:S(2)}, u32[]{:S(2)}) async-start(bf16[8,736,128]{2,1,0:T(8,128)(2,1)} %shard_map.159), calls=%async_computation.1 | async-start | bytes 3014656 | tf_op jit(solution)/shard_map/all_to_all | solution.py:550
  35.5 0.6 copy-done.11
  36.2 6.6 %shard_map.161 = (bf16[448,512]{1,0:T(8,128)(2,1)}, bf16[448,512]{1,0:T(8,128)(2,1)}, bf16[448,512]{1,0:T(8,128)(2,1)}, bf16[576,512]{1,0:T(8,128)(2,1)}) custom-call(bf16[704,512]{1,0:T(8,128)(2,1)} %get-tuple-element.30.ordered_t_in.refs_1_, f32[4,128,512]{2,1,0:T(8,128)} %get-tuple-element.31.nd_in, bf16[4,160,128]{2,1,0:T(8,128)(2,1)} %copy-done.11, ...), custom_call_target="tpu_custom_call" | custom-call | flops 10569646080 | bytes 36700160 | tf_op jit(solution)/shard_map/pallas_call | solution.py:727
  42.8 1.8 %collective-permute-start.4 = (bf16[448,512]{1,0:T(8,128)(2,1)}, bf16[448,512]{1,0:T(8,128)(2,1)S(1)}, u32[]{:S(2)}, u32[]{:S(2)}) collective-permute-start(bf16[448,512]{1,0:T(8,128)(2,1)} %get-tuple-element.38), channel_id=1, source_target_pairs={{0,1},{1,2},{4,5},{5,6},{8,9},{9,10},{12,13},{13,14},{16,17},{17,1... | collective-permute-start | bytes 1376264 | tf_op jit(solution)/shard_map/ppermute | solution.py:566
  44.6 0.7 collective-permute-start.5
  45.3 3.5 %collective-permute-start.6 = (bf16[448,512]{1,0:T(8,128)(2,1)}, bf16[448,512]{1,0:T(8,128)(2,1)S(1)}, u32[]{:S(2)}, u32[]{:S(2)}) collective-permute-start(bf16[448,512]{1,0:T(8,128)(2,1)} %get-tuple-element.40), channel_id=1, source_target_pairs={{0,3},{3,0},{4,7},{7,4},{8,11},{11,8},{12,15},{15,12},{16,19},{19,... | collective-permute-start | bytes 1376264 | tf_op jit(solution)/shard_map/ppermute | solution.py:574
  48.8 3.9 %shard_map.162 = (bf16[448,512]{1,0:T(8,128)(2,1)}, bf16[448,512]{1,0:T(8,128)(2,1)}, bf16[448,512]{1,0:T(8,128)(2,1)}) custom-call(bf16[448,1792]{1,0:T(8,128)(2,1)} %w_out_in.5, bf16[128,1792]{1,0:T(8,128)(2,1)} %w_up_in.5, bf16[576,512]{1,0:T(8,128)(2,1)} %get-tuple-element.36.inputs_in.refs_2_), custom_call_target="tpu_custom_call" | custom-call | flops 1 | bytes 1 | tf_op jit(solution)/shard_map/pallas_call | solution.py:744
  52.7 4.5 %shard_map.163 = f32[4,512]{1,0:T(4,128)} custom-call(bf16[512,576]{1,0:T(8,128)(2,1)} %get-tuple-element.41.refs_0_, bf16[704,512]{1,0:T(8,128)(2,1)} %get-tuple-element.30.ordered_t_in.refs_1_, bf16[4,160,128]{2,1,0:T(8,128)(2,1)} %copy-done.11, s32[1,512]{1,0:T(1,128)} %bitcast.7, bf16[160,16]{1,0:T(8,128)(2,1)} %constant.14.clone.left.refs_4_, ...), custom_call_target="tpu_custom_call" | custom-call | flops 1 | bytes 1 | tf_op jit(solution)/shard_map/pallas_call | solution.py:127
  57.2 2.3 %shard_map.164 = bf16[4,512,128]{2,1,0:T(8,128)(2,1)} custom-call(s32[128]{0:T(128)S(1)} %copy-done.8, bf16[8,736,128]{2,1,0:T(8,128)(2,1)S(1)} %all-to-all-done.1.refs_1_, bf16[576,512]{1,0:T(8,128)(2,1)S(1)} %copy-done.1), custom_call_target="tpu_custom_call" | custom-call | flops 1 | bytes 1 | tf_op jit(solution)/shard_map/pallas_call | solution.py:127
  59.6 3.6 %all-to-all-start.2 = ((bf16[4,512,128]{2,1,0:T(8,128)(2,1)}), bf16[4,512,128]{2,1,0:T(8,128)(2,1)S(1)}, u32[]{:S(2)}, u32[]{:S(2)}) async-start(bf16[4,512,128]{2,1,0:T(8,128)(2,1)} %shard_map.164), calls=%async_computation.2 | async-start | bytes 1048576 | tf_op jit(solution)/shard_map/all_to_all | solution.py:550
  63.2 4.9 %collective-permute-done.6 = bf16[448,512]{1,0:T(8,128)(2,1)S(1)} collective-permute-done((bf16[448,512]{1,0:T(8,128)(2,1)}, bf16[448,512]{1,0:T(8,128)(2,1)S(1)}, u32[]{:S(2)}, u32[]{:S(2)}) %collective-permute-start.6) | collective-permute-done | bytes 458784 | tf_op jit(solution)/shard_map/ppermute | solution.py:574
  68.1 1.1 %add_convert_fusion.2 = bf16[448,512]{1,0:T(8,128)(2,1)S(1)} fusion(bf16[448,512]{1,0:T(8,128)(2,1)S(1)} %collective-permute-done.4, bf16[448,512]{1,0:T(8,128)(2,1)} %get-tuple-element.44), kind=kLoop, calls=%fused_computation.2 | loop fusion | flops 917504 | bytes 1376256 | tf_op jit(solution)/shard_map/convert_element_type | solution.py:563
  69.3 6.4 %collective-permute-start.7 = (bf16[448,512]{1,0:T(8,128)(2,1)S(1)}, bf16[448,512]{1,0:T(8,128)(2,1)S(1)}, u32[]{:S(2)}, u32[]{:S(2)}) collective-permute-start(bf16[448,512]{1,0:T(8,128)(2,1)S(1)} %add_convert_fusion.2), channel_id=1, source_target_pairs={{0,1},{1,2},{2,3},{4,5},{5,6},{6,7},{8,9},{9,10},{10,11},{12,13},{... | collective-permute-start | bytes 1376264 | tf_op jit(solution)/shard_map/ppermute | solution.py:566
  75.7 0.1 add_convert_fusion.1
  75.8 1.3 %collective-permute-start.8 = (bf16[448,512]{1,0:T(8,128)(2,1)S(1)}, bf16[448,512]{1,0:T(8,128)(2,1)S(1)}, u32[]{:S(2)}, u32[]{:S(2)}) collective-permute-start(bf16[448,512]{1,0:T(8,128)(2,1)S(1)} %add_convert_fusion.1), channel_id=1, source_target_pairs={{1,0},{2,1},{3,2},{5,4},{6,5},{7,6},{9,8},{10,9},{11,10},{13,12},{... | collective-permute-start | bytes 1376264 | tf_op jit(solution)/shard_map/ppermute | solution.py:569
  77.1 8.9 %collective-permute-done.7 = bf16[448,512]{1,0:T(8,128)(2,1)S(1)} collective-permute-done((bf16[448,512]{1,0:T(8,128)(2,1)S(1)}, bf16[448,512]{1,0:T(8,128)(2,1)S(1)}, u32[]{:S(2)}, u32[]{:S(2)}) %collective-permute-start.7) | collective-permute-done | bytes 458784 | tf_op jit(solution)/shard_map/ppermute | solution.py:566
  86.0 4.4 %collective-permute-done.8 = bf16[448,512]{1,0:T(8,128)(2,1)S(1)} collective-permute-done((bf16[448,512]{1,0:T(8,128)(2,1)S(1)}, bf16[448,512]{1,0:T(8,128)(2,1)S(1)}, u32[]{:S(2)}, u32[]{:S(2)}) %collective-permute-start.8) | collective-permute-done | bytes 458784 | tf_op jit(solution)/shard_map/ppermute | solution.py:569
  90.5 1.0 %fusion = bf16[512,448]{0,1:T(8,128)(2,1)} fusion(bf16[448,512]{1,0:T(8,128)(2,1)S(1)} %collective-permute-done.8, bf16[448,512]{1,0:T(8,128)(2,1)S(1)} %collective-permute-done.7, bf16[448,512]{1,0:T(8,128)(2,1)S(1)} %collective-permute-done.6, bf16[448,512]{1,0:T(8,128)(2,1)S(1)} %copy-done.9), kind=kLoop, calls=%fused_computation.3 | loop fusion | flops 1835008 | bytes 2293760 | tf_op jit(solution)/shard_map/transpose | solution.py:798
  91.5 0.6 shard_map.165
  (35 shorter events, 0.1 us)
Async XLA Ops:
  0.6 11.4 %copy-start.4 = (bf16[16,1792]{1,0:T(8,128)(2,1)S(1)}, bf16[16,1792]{1,0:T(8,128)(2,1)}, u32[]{:S(2)}) copy-start(bf16[16,1792]{1,0:T(8,128)(2,1)} %refs_3_) | copy-start | bytes 172036
  0.6 17.0 %copy-start.12 = (s32[32]{0:T(128)S(1)}, s32[32]{0:T(128)}, u32[]{:S(2)}) copy-start(s32[32]{0:T(128)} %param.23) | copy-start | bytes 388
  0.7 17.0 %copy-start.13 = (s32[32]{0:T(128)S(1)}, s32[32]{0:T(128)}, u32[]{:S(2)}) copy-start(s32[32]{0:T(128)} %param.22) | copy-start | bytes 388
  0.7 17.2 %copy-start.7 = (s32[512]{0:T(512)S(1)}, s32[512]{0:T(512)}, u32[]{:S(2)}) copy-start(s32[512]{0:T(512)} %param.21) | copy-start | bytes 6148
  6.9 17.7 %all-to-all-start = ((bf16[8,352,128]{2,1,0:T(8,128)(2,1)}), bf16[8,352,128]{2,1,0:T(8,128)(2,1)S(1)}, u32[]{:S(2)}, u32[]{:S(2)}) async-start(bf16[8,352,128]{2,1,0:T(8,128)(2,1)} %shard_map.157), calls=%async_computation | async-start | bytes 1441792 | tf_op jit(solution)/shard_map/all_to_all | solution.py:550
  12.1 9.4 %collective-permute-start.2 = (bf16[16,1792]{1,0:T(8,128)(2,1)S(1)}, bf16[16,1792]{1,0:T(8,128)(2,1)S(1)}, u32[]{:S(2)}, u32[]{:S(2)}) collective-permute-start(bf16[16,1792]{1,0:T(8,128)(2,1)S(1)} %copy-done.4), channel_id=1, source_target_pairs={{0,1},{1,2},{2,3},{3,0},{4,5},{5,6},{6,7},{7,4},{8,9},{9,10},{10,1... | collective-permute-start | bytes 172040 | tf_op jit(solution)/shard_map/ppermute | solution.py:555
  13.7 7.8 %collective-permute-start.1 = (bf16[16,1792]{1,0:T(8,128)(2,1)S(1)}, bf16[16,1792]{1,0:T(8,128)(2,1)S(1)}, u32[]{:S(2)}, u32[]{:S(2)}) collective-permute-start(bf16[16,1792]{1,0:T(8,128)(2,1)S(1)} %copy-done.4), channel_id=1, source_target_pairs={{0,2},{1,3},{2,0},{3,1},{4,6},{5,7},{6,4},{7,5},{8,10},{9,11},{10,... | collective-permute-start | bytes 172040 | tf_op jit(solution)/shard_map/ppermute | solution.py:555
  16.3 5.2 %collective-permute-start = (bf16[16,1792]{1,0:T(8,128)(2,1)S(1)}, bf16[16,1792]{1,0:T(8,128)(2,1)S(1)}, u32[]{:S(2)}, u32[]{:S(2)}) collective-permute-start(bf16[16,1792]{1,0:T(8,128)(2,1)S(1)} %copy-done.4), channel_id=1, source_target_pairs={{0,3},{1,0},{2,1},{3,2},{4,7},{5,4},{6,5},{7,6},{8,11},{9,8},{10,9... | collective-permute-start | bytes 172040 | tf_op jit(solution)/shard_map/ppermute | solution.py:555
  18.5 3.0 %copy-start = (bf16[448,1792]{1,0:T(8,128)(2,1)S(1)}, bf16[448,1792]{1,0:T(8,128)(2,1)}, u32[]{:S(2)}) copy-start(bf16[448,1792]{1,0:T(8,128)(2,1)} %w_out_in.5) | copy-start | bytes 4816900
  18.5 3.0 %copy-start.2 = (bf16[128,1792]{1,0:T(8,128)(2,1)S(1)}, bf16[128,1792]{1,0:T(8,128)(2,1)}, u32[]{:S(2)}) copy-start(bf16[128,1792]{1,0:T(8,128)(2,1)} %w_up_in.5) | copy-start | bytes 1376260
  21.4 3.2 %copy-start.3 = (f32[160,8]{1,0:T(8,128)S(1)}, f32[160,8]{1,0:T(8,128)}, u32[]{:S(2)}) copy-start(f32[160,8]{1,0:T(8,128)} %constant.16.clone.cols.refs_6_) | copy-start | bytes 15364
  21.4 3.2 %copy-start.5 = (bf16[160,16]{1,0:T(8,128)(2,1)S(1)}, bf16[160,16]{1,0:T(8,128)(2,1)}, u32[]{:S(2)}) copy-start(bf16[160,16]{1,0:T(8,128)(2,1)} %constant.15.clone.right.refs_5_) | copy-start | bytes 15364
  21.4 3.2 %copy-start.6 = (bf16[160,16]{1,0:T(8,128)(2,1)S(1)}, bf16[160,16]{1,0:T(8,128)(2,1)}, u32[]{:S(2)}) copy-start(bf16[160,16]{1,0:T(8,128)(2,1)} %constant.14.clone.left.refs_4_) | copy-start | bytes 15364
  21.4 3.2 %copy-start.8 = (s32[128]{0:T(128)S(1)}, s32[128]{0:T(128)}, u32[]{:S(2)}) copy-start(s32[128]{0:T(128)} %refs_0_.1) | copy-start | bytes 1540
  29.2 6.4 %collective-permute-start.3 = (bf16[4,160,128]{2,1,0:T(8,128)(2,1)}, bf16[4,160,128]{2,1,0:T(8,128)(2,1)S(1)}, u32[]{:S(2)}, u32[]{:S(2)}) collective-permute-start(bf16[4,160,128]{2,1,0:T(8,128)(2,1)} %get-tuple-element.34), channel_id=1, source_target_pairs={{0,4},{4,8},{8,12},{12,16},{16,20},{20,24},{24,28},{1,5},{5,9},{9,... | collective-permute-start | bytes 491528 | tf_op jit(solution)/shard_map/ppermute | solution.py:723
  30.7 26.5 %all-to-all-start.1 = ((bf16[8,736,128]{2,1,0:T(8,128)(2,1)}), bf16[8,736,128]{2,1,0:T(8,128)(2,1)S(1)}, u32[]{:S(2)}, u32[]{:S(2)}) async-start(bf16[8,736,128]{2,1,0:T(8,128)(2,1)} %shard_map.159), calls=%async_computation.1 | async-start | bytes 3014656 | tf_op jit(solution)/shard_map/all_to_all | solution.py:550
  35.5 0.7 copy-start.11
  42.8 20.4 %collective-permute-start.4 = (bf16[448,512]{1,0:T(8,128)(2,1)}, bf16[448,512]{1,0:T(8,128)(2,1)S(1)}, u32[]{:S(2)}, u32[]{:S(2)}) collective-permute-start(bf16[448,512]{1,0:T(8,128)(2,1)} %get-tuple-element.38), channel_id=1, source_target_pairs={{0,1},{1,2},{4,5},{5,6},{8,9},{9,10},{12,13},{13,14},{16,17},{17,1... | collective-permute-start | bytes 1376264 | tf_op jit(solution)/shard_map/ppermute | solution.py:566
  44.6 18.6 %collective-permute-start.5 = (bf16[448,512]{1,0:T(8,128)(2,1)}, bf16[448,512]{1,0:T(8,128)(2,1)S(1)}, u32[]{:S(2)}, u32[]{:S(2)}) collective-permute-start(bf16[448,512]{1,0:T(8,128)(2,1)} %get-tuple-element.39), channel_id=1, source_target_pairs={{2,1},{3,2},{6,5},{7,6},{10,9},{11,10},{14,13},{15,14},{18,17},{19... | collective-permute-start | bytes 1376264 | tf_op jit(solution)/shard_map/ppermute | solution.py:569
  45.3 22.8 %collective-permute-start.6 = (bf16[448,512]{1,0:T(8,128)(2,1)}, bf16[448,512]{1,0:T(8,128)(2,1)S(1)}, u32[]{:S(2)}, u32[]{:S(2)}) collective-permute-start(bf16[448,512]{1,0:T(8,128)(2,1)} %get-tuple-element.40), channel_id=1, source_target_pairs={{0,3},{3,0},{4,7},{7,4},{8,11},{11,8},{12,15},{15,12},{16,19},{19,... | collective-permute-start | bytes 1376264 | tf_op jit(solution)/shard_map/ppermute | solution.py:574
  48.8 8.5 %copy-start.1 = (bf16[576,512]{1,0:T(8,128)(2,1)S(1)}, bf16[576,512]{1,0:T(8,128)(2,1)}, u32[]{:S(2)}) copy-start(bf16[576,512]{1,0:T(8,128)(2,1)} %get-tuple-element.36.inputs_in.refs_2_) | copy-start | bytes 1769476
  59.6 16.1 %copy-start.10 = (bf16[448,512]{1,0:T(8,128)(2,1)S(1)}, bf16[448,512]{1,0:T(8,128)(2,1)}, u32[]{:S(2)}) copy-start(bf16[448,512]{1,0:T(8,128)(2,1)} %get-tuple-element.46) | copy-start | bytes 1376260
  59.6 31.9 %all-to-all-start.2 = ((bf16[4,512,128]{2,1,0:T(8,128)(2,1)}), bf16[4,512,128]{2,1,0:T(8,128)(2,1)S(1)}, u32[]{:S(2)}, u32[]{:S(2)}) async-start(bf16[4,512,128]{2,1,0:T(8,128)(2,1)} %shard_map.164), calls=%async_computation.2 | async-start | bytes 1048576 | tf_op jit(solution)/shard_map/all_to_all | solution.py:550
  63.2 27.2 %copy-start.9 = (bf16[448,512]{1,0:T(8,128)(2,1)S(1)}, bf16[448,512]{1,0:T(8,128)(2,1)}, u32[]{:S(2)}) copy-start(bf16[448,512]{1,0:T(8,128)(2,1)} %get-tuple-element.37) | copy-start | bytes 1376260
  69.3 16.8 %collective-permute-start.7 = (bf16[448,512]{1,0:T(8,128)(2,1)S(1)}, bf16[448,512]{1,0:T(8,128)(2,1)S(1)}, u32[]{:S(2)}, u32[]{:S(2)}) collective-permute-start(bf16[448,512]{1,0:T(8,128)(2,1)S(1)} %add_convert_fusion.2), channel_id=1, source_target_pairs={{0,1},{1,2},{2,3},{4,5},{5,6},{6,7},{8,9},{9,10},{10,11},{12,13},{... | collective-permute-start | bytes 1376264 | tf_op jit(solution)/shard_map/ppermute | solution.py:566
  75.8 14.7 %collective-permute-start.8 = (bf16[448,512]{1,0:T(8,128)(2,1)S(1)}, bf16[448,512]{1,0:T(8,128)(2,1)S(1)}, u32[]{:S(2)}, u32[]{:S(2)}) collective-permute-start(bf16[448,512]{1,0:T(8,128)(2,1)S(1)} %add_convert_fusion.1), channel_id=1, source_target_pairs={{1,0},{2,1},{3,2},{5,4},{6,5},{7,6},{9,8},{10,9},{11,10},{13,12},{... | collective-permute-start | bytes 1376264 | tf_op jit(solution)/shard_map/ppermute | solution.py:569
where the time goes:
time: 92.7 us; the launch traced here: 92.1 us
  Pallas kernels  34.6 us (37%)
  starting transfers between devices  34.4 us (37%)
  waiting for transfers between devices  18.3 us (20%)
  other arithmetic  3.11 us (3%)
  between operations  0.99 us (1%)
    all_to_all x3, starting transfers between devices, exchange(): return lax.all_to_all(blocks, axis, split_axis=0, concat_axis=0, tiled=True)  13.6 us
    ppermute x2, waiting for transfers between devices, up(): return lax.ppermute(values, axis, [(i, i + 1) for i in range(first, last)])  8.95 us
    ppermute x2, starting transfers between devices, up(): return lax.ppermute(values, axis, [(i, i + 1) for i in range(first, last)])  8.2 us
    pallas_call x2, Pallas kernels, staged_call(): kernel_call(run, [pltpu.HBM(x.shape, x.dtype) for x in out_shape], [SMEM]...  6.83 us
    pallas_call x1, Pallas kernels, on_device(): kernel_call(functools.partial(finish_kernel, low, heads, shards), [part]...  6.58 us
    pallas_call x1, Pallas kernels, on_device(): kernel_call(functools.partial(project_kernel, dims), pltpu.HBM((groups, p...  6.19 us
    ppermute x3, starting transfers between devices, ring_rows(): lax.ppermute(values, axis, [(i, (i + by) % size) for i in range(size)])  5.57 us
    ppermute x1, waiting for transfers between devices, line_sums(): far = lax.ppermute(terms[3], axis, [(0, 3), (3, 0)])  4.87 us
  transfers between devices with their start and end apart: 12, of which 3 were waited for; matrix products, arithmetic and copies ran while one was open for 3% of the time, Pallas kernels for 25%

commit v1 on v0

--- a/solution.py
+++ b/solution.py
@@ -17,7 +17,6 @@
 PHI_PAD = 160
 LANES = 128
 ONE, TAG, REST = HD, HD + 1, HD + 2
-NEAR = (0, 1, -1)
 MIB = 1024 * 1024
 VMEM_LIMIT = 60 * MIB
 
@@ -367,15 +366,35 @@
     return max(-(-(j * width % LANES + width) // LANES) * LANES for j in range(shards))
 
 
-def each_shard(offsets, shards):
-    for k, offset in enumerate(offsets):
-        for own in range(shards):
-            if 0 <= own + offset < shards:
-                yield k, own, own + offset
-
-
-def shard_parts(offsets, shards, w_out_in, w_up_in, weights, w_sems, inputs, held_out, outs, sems):
+def far_tables(shards):
+    if shards == 4:
+        return [(3, 3, 0, 0), (2, None, None, 1)]
+    tables = [tuple({0: shards - 1, shards - 1: 0}.get(own) for own in range(shards))]
+    for distance in range(shards - 2, 1, -1):
+        tables += [offset_table(distance, shards), offset_table(-distance, shards)]
+    return tables
+
+
+def near_tables(shards):
+    if shards == 4:
+        return [(0, 1, 2, 3), (1, 0, 3, 2), (None, 2, 1, None)]
+    return [offset_table(offset, shards) for offset in (0, 1, -1)]
+
+
+def offset_table(offset, shards):
+    return tuple(own + offset if 0 <= own + offset < shards else None for own in range(shards))
+
+
+def each_shard(tables):
+    for k, table in enumerate(tables):
+        for own, j in enumerate(table):
+            if j is not None:
+                yield k, own, j
+
+
+def shard_parts(tables, w_out_in, w_up_in, weights, w_sems, inputs, held_out, outs, sems):
     own_shard = lax.axis_index("mp")
+    shards = len(tables[0])
     inner, model_width = w_out_in.shape
     width = model_width // shards
 
@@ -389,7 +408,7 @@
         )
 
     def fetch():
-        for k, own, j in each_shard(offsets, shards):
+        for k, own, j in each_shard(tables):
 
             @pl.when(own_shard == own)
             def _(k=k, j=j):
@@ -397,7 +416,7 @@
                     copy.start()
 
     def compute():
-        for k, own, j in each_shard(offsets, shards):
+        for k, own, j in each_shard(tables):
 
             @pl.when(own_shard == own)
             def _(k=k, j=j):
@@ -408,7 +427,7 @@
                 start(held_out.at[k], outs[k], sems.at[k])
 
     def finish():
-        for k, own, j in each_shard(offsets, shards):
+        for k, own, j in each_shard(tables):
 
             @pl.when(own_shard == own)
             def _(k=k):
@@ -420,12 +439,11 @@
 def finish_kernel(
     low, heads, shards, ordered_t_in, nd_in, state, segrow, slotrow, left, right, cols, w_out_in, w_up_in, *refs
 ):
-    far = far_offsets(shards)
-    outs = refs[: len(far) - 1]
-    outs = [outs[0], *outs]
-    inputs_in, queries, nd, weights, inputs, held_out, sems, w_sems = refs[len(far) - 1 :]
+    far = far_tables(shards)
+    outs = refs[: len(far)]
+    inputs_in, state_in, queries, nd, weights, inputs, held_out, sems, w_sems = refs[len(far) :]
     inner = heads * HD
-    sem = iter(range(len(far), len(far) + 2 * heads + 2))
+    sem = iter(range(len(far), len(far) + 2 * heads + 3))
     lows = start(ordered_t_in.at[pl.ds(0, low)], inputs.at[pl.ds(inner, low)], sems.at[next(sem)])
     fetches = []
     for h in range(heads):
@@ -433,7 +451,7 @@
         fetches.append(start(ordered_t_in.at[rows], queries.at[h], sems.at[next(sem)]))
         fetches.append(start(nd_in.at[h], nd.at[h], sems.at[next(sem)]))
     fetch_weights, compute, finish = shard_parts(
-        far, shards, w_out_in, w_up_in, weights, w_sems, inputs, held_out, outs, sems
+        far, w_out_in, w_up_in, weights, w_sems, inputs, held_out, outs, sems
     )
     fetch_weights()
     tag, _ = state_corner(state)
@@ -449,23 +467,18 @@
         both = nd[h] + carried * cross
         inputs[h * HD : (h + 1) * HD, :] = (both[:HD, :] / both[ONE : ONE + 1, :]).astype(BF)
     compute()
-    kept = start(inputs, inputs_in, sems.at[next(sem)])
+    kept = [start(inputs, inputs_in, sems.at[next(sem)]), start(state, state_in, sems.at[next(sem)])]
     finish()
-    kept.wait()
-
-
-def far_offsets(shards):
-    far = [shards - 1, 1 - shards]
-    for distance in range(shards - 2, 1, -1):
-        far += [distance, -distance]
-    return far
+    for copy in kept:
+        copy.wait()
 
 
 def near_kernel(shards, w_out_in, w_up_in, inputs_in, *refs):
-    outs = refs[: len(NEAR)]
-    weights, inputs, held_out, sems, w_sems = refs[len(NEAR) :]
-    load = start(inputs_in, inputs, sems.at[len(NEAR)])
-    fetch, compute, finish = shard_parts(NEAR, shards, w_out_in, w_up_in, weights, w_sems, inputs, held_out, outs, sems)
+    near = near_tables(shards)
+    outs = refs[: len(near)]
+    weights, inputs, held_out, sems, w_sems = refs[len(near) :]
+    load = start(inputs_in, inputs, sems.at[len(near)])
+    fetch, compute, finish = shard_parts(near, w_out_in, w_up_in, weights, w_sems, inputs, held_out, outs, sems)
     fetch()
     load.wait()
     compute()
@@ -556,26 +569,29 @@
     return [*steps, values]
 
 
-def line_sums(terms, axis, beside):
+def line_sums(far_terms, near_terms, axis, beside):
     size = lax.axis_size(axis)
 
     def joined(*parts):
         return sum(part.astype(F32) for part in parts).astype(BF)
 
-    def up(values, first, last):
-        return lax.ppermute(values, axis, [(i, i + 1) for i in range(first, last)])
-
-    def down(values, first, last):
-        return lax.ppermute(values, axis, [(i, i - 1) for i in range(first, last)])
-
+    def send(values, *pairs):
+        return lax.ppermute(values, axis, pairs)
+
+    own_term = near_terms[0]
     if size == 4:
-        relayed_up = up(terms[2], 0, size - 2)
-        relayed_down = down(terms[-2], 2, size)
-        far = lax.ppermute(terms[3], axis, [(0, 3), (3, 0)])
-        relayed_up, relayed_down, far, beside = lax.optimization_barrier((relayed_up, relayed_down, far, beside))
-        near_up = up(joined(terms[1], relayed_up), 0, size - 1)
-        near_down = down(joined(terms[-1], relayed_down), 1, size)
-        return joined(terms[0], far, near_up, near_down), beside
+        here = lax.axis_index(axis)
+        middle = (here == 1) | (here == 2)
+        across = send(far_terms[0], (1, 2), (2, 1), (0, 3), (3, 0))
+        inward = send(far_terms[1], (0, 1), (3, 2))
+        across, inward, beside = lax.optimization_barrier((across, inward, beside))
+        relayed = jnp.where(middle, across, 0)
+        paired = send(joined(near_terms[1], relayed), (0, 1), (1, 0), (2, 3), (3, 2))
+        centre = send(joined(near_terms[2], inward), (1, 2), (2, 1))
+        return joined(own_term, jnp.where(middle, centre, across), paired), beside
+    terms = {1: near_terms[1], -1: near_terms[2], size - 1: far_terms[0], 1 - size: far_terms[0]}
+    for distance in range(size - 2, 1, -1):
+        terms[distance], terms[-distance] = far_terms[2 * (size - 1 - distance) - 1 :][:2]
     going_up = going_down = None
     for step in range(1, size):
         to_up = terms[size - step]
@@ -583,9 +599,9 @@
         if step > 1:
             to_up = joined(to_up, going_up)
             to_down = joined(to_down, going_down)
-        going_up = up(to_up, 0, step)
-        going_down = down(to_down, size - step, size)
-    return joined(terms[0], going_up, going_down), beside
+        going_up = send(to_up, *[(i, i + 1) for i in range(step)])
+        going_down = send(to_down, *[(i, i - 1) for i in range(size - step, size)])
+    return joined(own_term, going_up, going_down), beside
 
 
 def on_device(
@@ -722,41 +738,41 @@
     beside = exchange(beside, "group")
     state = lax.ppermute(state, "group", [(i, i + 1) for i in range(groups - 1)])
 
-    far = far_offsets(shards)
+    far, near = len(far_tables(shards)), len(near_tables(shards))
     part = pltpu.HBM((width, count), BF)
-    *far_terms, inputs = kernel_call(
+    *far_terms, inputs, kept_state = kernel_call(
         functools.partial(finish_kernel, low, heads, shards),
-        [part] * (len(far) - 1) + [pltpu.HBM((inner + low, count), BF)],
+        [part] * far + [pltpu.HBM((inner + low, count), BF), pltpu.HBM((heads, PHI_PAD, LANES), BF)],
         [ANY] * 2 + [VMEM] * 6 + [ANY] * 2,
-        [ANY] * len(far),
+        [ANY] * (far + 2),
         [
             pltpu.VMEM((heads, FEAT, count), BF),
             pltpu.VMEM((heads, LANES, count), F32),
-            pltpu.VMEM((len(far), inner + low, window), BF),
+            pltpu.VMEM((far, inner + low, window), BF),
             pltpu.VMEM((inner + low, count), BF),
-            pltpu.VMEM((len(far), width, count), BF),
-            dma((len(far) + 2 * heads + 2,)),
-            dma((2 * len(far),)),
+            pltpu.VMEM((far, width, count), BF),
+            dma((far + 2 * heads + 3,)),
+            dma((2 * far,)),
         ],
         20 * count * (inner + low) * model_width,
         40 * count * model_width,
     )(ordered_t, nd, state, segrow, slotrow, left, right, cols, out_weight, adapter_up)
     near_terms = kernel_call(
         functools.partial(near_kernel, shards),
-        [part] * len(NEAR),
+        [part] * near,
         [ANY] * 3,
-        [ANY] * len(NEAR),
+        [ANY] * near,
         [
-            pltpu.VMEM((len(NEAR), inner + low, window), BF),
+            pltpu.VMEM((near, inner + low, window), BF),
             pltpu.VMEM((inner + low, count), BF),
-            pltpu.VMEM((len(NEAR), width, count), BF),
-            dma((len(NEAR) + 1,)),
-            dma((2 * len(NEAR),)),
+            pltpu.VMEM((near, width, count), BF),
+            dma((near + 1,)),
+            dma((2 * near,)),
         ],
         1,
         1,
     )(out_weight, adapter_up, inputs)
-    terms = dict(zip(NEAR, near_terms)) | dict(zip(far, [far_terms[0], *far_terms]))
+
     [logits] = staged_call(
         functools.partial(logits_kernel, dims, shards, width),
         [shape((shards, scored, count // shards), BF)],
@@ -778,12 +794,12 @@
         functools.partial(norms_kernel, low, heads),
         [shape((heads, count), F32)],
         [],
-        [ordered, ordered_t, state, segrow, left, right, cols],
+        [ordered, ordered_t, kept_state, segrow, left, right, cols],
         [pltpu.VMEM((count, count), F32)],
         1,
         1,
     )
-    update, [state_norms, _] = line_sums(terms, "mp", [state_norms, logits])
+    update, [state_norms, _] = line_sums(far_terms, near_terms, "mp", [state_norms, logits])
     logits = exchange(logits, "mp")
     best = kernel_call(
         functools.partial(best_kernel, shards),

time: 92.7 us -> 86.7 us (0.935)
  starting transfers between devices: 34.4 us -> 27.1 us
  waiting for transfers between devices: 18.3 us -> 19.9 us
  other arithmetic: 3.11 us -> 2.11 us
    ppermute x5 -> x4, starting transfers between devices: 13.6 us -> 6.36 us  [send(): return lax.ppermute(values, axis, pairs)]
    all_to_all x3, waiting for transfers between devices: 0.01 us -> 1.46 us  [exchange(): return lax.all_to_all(blocks, axis, split_axis=0, concat_axis=0, tiled=True)]
    convert_element_type x2, other arithmetic: 1.26 us -> 0.26 us  [joined(): return sum((part.astype(F32) for part in parts)).astype(BF)]
    ppermute x5 -> x4, waiting for transfers between devices: 18.2 us -> 18.4 us  [send(): return lax.ppermute(values, axis, pairs)]
  transfers between devices with their start and end apart: 12 -> 11, of which waited for: 3 -> 3; matrix products, arithmetic and copies ran while one was open for 3% -> 2% of each run, Pallas kernels for 25% -> 27%
where the time goes in v1:
time: 86.7 us; the launch traced here: 85.3 us
  Pallas kernels  34.5 us (40%)
  starting transfers between devices  27.1 us (31%)
  waiting for transfers between devices  19.9 us (23%)
  other arithmetic  2.11 us (2%)
  between operations  0.96 us (1%)
    ppermute x4, waiting for transfers between devices, send(): return lax.ppermute(values, axis, pairs)  18.4 us
    all_to_all x3, starting transfers between devices, exchange(): return lax.all_to_all(blocks, axis, split_axis=0, concat_axis=0, tiled=True)  13.6 us
    pallas_call x2, Pallas kernels, staged_call(): kernel_call(run, [pltpu.HBM(x.shape, x.dtype) for x in out_shape], [SMEM]...  6.83 us
    pallas_call x1, Pallas kernels, on_device(): kernel_call(functools.partial(finish_kernel, low, heads, shards), [part]...  6.45 us
    ppermute x4, starting transfers between devices, send(): return lax.ppermute(values, axis, pairs)  6.36 us
    pallas_call x1, Pallas kernels, on_device(): kernel_call(functools.partial(project_kernel, dims), pltpu.HBM((groups, p...  6.19 us
    ppermute x3, starting transfers between devices, ring_rows(): lax.ppermute(values, axis, [(i, (i + by) % size) for i in range(size)])  5.57 us
    pallas_call x1, Pallas kernels, on_device(): kernel_call(functools.partial(group_kernel, dims, low, heads), (pltpu.HBM...  4.49 us
  transfers between devices with their start and end apart: 11, of which 3 were waited for; matrix products, arithmetic and copies ran while one was open for 2% of the time, Pallas kernels for 27%

profile of v1, /device:TPU:0, one launch (start us, length us, event | category | flops | bytes accessed | tf_op | source)
XLA Modules:
  0.0 85.3 jit_solution(13720417032727184741)
XLA Ops:
  0.7 6.2 %shard_map.157 = bf16[8,352,128]{2,1,0:T(8,128)(2,1)} custom-call(s32[128]{0:T(128)} %refs_0_.1, bf16[512,1792]{1,0:T(8,128)(2,1)} %hidden_in.2, f32[1792]{0:T(1024)} %gain.1, bf16[576,1792]{1,0:T(8,128)(2,1)} %bitcast.9, bf16[1792,128]{1,0:T(8,128)(2,1)} %wd_in.1), custom_call_target="tpu_custom_call" | custom-call | flops 1291845632 | bytes 4358144 | tf_op jit(solution)/shard_map/pallas_call | solution.py:648
  6.9 5.2 %all-to-all-start = ((bf16[8,352,128]{2,1,0:T(8,128)(2,1)}), bf16[8,352,128]{2,1,0:T(8,128)(2,1)S(1)}, u32[]{:S(2)}, u32[]{:S(2)}) async-start(bf16[8,352,128]{2,1,0:T(8,128)(2,1)} %shard_map.157), calls=%async_computation | async-start | bytes 1441792 | tf_op jit(solution)/shard_map/all_to_all | solution.py:563
  12.1 1.6 %collective-permute-start.2 = (bf16[16,1792]{1,0:T(8,128)(2,1)S(1)}, bf16[16,1792]{1,0:T(8,128)(2,1)S(1)}, u32[]{:S(2)}, u32[]{:S(2)}) collective-permute-start(bf16[16,1792]{1,0:T(8,128)(2,1)S(1)} %copy-done.4), channel_id=1, source_target_pairs={{0,1},{1,2},{2,3},{3,0},{4,5},{5,6},{6,7},{7,4},{8,9},{9,10},{10,1... | collective-permute-start | bytes 172040 | tf_op jit(solution)/shard_map/ppermute | solution.py:568
  13.7 2.6 %collective-permute-start.1 = (bf16[16,1792]{1,0:T(8,128)(2,1)S(1)}, bf16[16,1792]{1,0:T(8,128)(2,1)S(1)}, u32[]{:S(2)}, u32[]{:S(2)}) collective-permute-start(bf16[16,1792]{1,0:T(8,128)(2,1)S(1)} %copy-done.4), channel_id=1, source_target_pairs={{0,2},{1,3},{2,0},{3,1},{4,6},{5,7},{6,4},{7,5},{8,10},{9,11},{10,... | collective-permute-start | bytes 172040 | tf_op jit(solution)/shard_map/ppermute | solution.py:568
  16.3 1.4 %collective-permute-start = (bf16[16,1792]{1,0:T(8,128)(2,1)S(1)}, bf16[16,1792]{1,0:T(8,128)(2,1)S(1)}, u32[]{:S(2)}, u32[]{:S(2)}) collective-permute-start(bf16[16,1792]{1,0:T(8,128)(2,1)S(1)} %copy-done.4), channel_id=1, source_target_pairs={{0,3},{1,0},{2,1},{3,2},{4,7},{5,4},{6,5},{7,6},{8,11},{9,8},{10,9... | collective-permute-start | bytes 172040 | tf_op jit(solution)/shard_map/ppermute | solution.py:568
  17.6 0.2 select_reduce_fusion.1
  17.8 0.1 select_reduce_fusion
  17.9 0.6 broadcast_subtract_fusion
  18.5 2.9 %shard_map.158.refs_4_ = bf16[8,736,128]{2,1,0:T(8,128)(2,1)} custom-call(s32[128]{0:T(128)} %refs_0_.1, bf16[512,1792]{1,0:T(8,128)(2,1)} %hidden_in.2), custom_call_target="tpu_custom_call" | custom-call | flops 1 | bytes 1 | tf_op jit(solution)/shard_map/pallas_call | solution.py:677
  21.4 0.0 copy-start.3
  21.4 0.0 copy-start.5
  21.5 3.1 %shard_map.159 = bf16[8,736,128]{2,1,0:T(8,128)(2,1)} custom-call(bf16[448,1792]{1,0:T(8,128)(2,1)S(1)} %copy-done, bf16[128,1792]{1,0:T(8,128)(2,1)S(1)} %copy-done.2, bf16[16,1792]{1,0:T(8,128)(2,1)S(1)} %collective-permute-done.refs_0_, bf16[16,1792]{1,0:T(8,128)(2,1)S(1)} %collective-permute-done.1.refs_1_, ...), custom_call_target="tpu_custom_call", output_to_operand_aliasing={{}: (6, {})} | custom-call | flops 132120576 | bytes 1835008 | tf_op jit(solution)/shard_map/pallas_call | solution.py:692
  24.7 4.5 %shard_map.160 = (bf16[512,576]{1,0:T(8,128)(2,1)}, bf16[704,512]{1,0:T(8,128)(2,1)}, bf16[4,160,128]{2,1,0:T(8,128)(2,1)}, f32[4,128,512]{2,1,0:T(8,128)}) custom-call(s32[128]{0:T(128)S(1)} %copy-done.8, bf16[8,352,128]{2,1,0:T(8,128)(2,1)S(1)} %all-to-all-done.arrived, s32[1,512]{1,0:T(1,128)S(1)} %bitcast.8, bf16[160,16]{1,0:T(8,128)(2,1)S(1)} %copy-done.6, ...), custom_call_target="tpu_custom_call" | custom-call | flops 1073741824 | bytes 2162688 | tf_op jit(solution)/shard_map/pallas_call | solution.py:712
  29.2 1.5 %collective-permute-start.3 = (bf16[4,160,128]{2,1,0:T(8,128)(2,1)}, bf16[4,160,128]{2,1,0:T(8,128)(2,1)S(1)}, u32[]{:S(2)}, u32[]{:S(2)}) collective-permute-start(bf16[4,160,128]{2,1,0:T(8,128)(2,1)} %get-tuple-element.33), channel_id=1, source_target_pairs={{0,4},{4,8},{8,12},{12,16},{16,20},{20,24},{24,28},{1,5},{5,9},{9,... | collective-permute-start | bytes 491528 | tf_op jit(solution)/shard_map/ppermute | solution.py:739
  30.7 4.8 %all-to-all-start.1 = ((bf16[8,736,128]{2,1,0:T(8,128)(2,1)}), bf16[8,736,128]{2,1,0:T(8,128)(2,1)S(1)}, u32[]{:S(2)}, u32[]{:S(2)}) async-start(bf16[8,736,128]{2,1,0:T(8,128)(2,1)} %shard_map.159), calls=%async_computation.1 | async-start | bytes 3014656 | tf_op jit(solution)/shard_map/all_to_all | solution.py:563
  35.5 0.7 copy-done.12
  36.2 6.5 %shard_map.161 = (bf16[448,512]{1,0:T(8,128)(2,1)}, bf16[448,512]{1,0:T(8,128)(2,1)}, bf16[576,512]{1,0:T(8,128)(2,1)}, bf16[4,160,128]{2,1,0:T(8,128)(2,1)}) custom-call(bf16[704,512]{1,0:T(8,128)(2,1)} %get-tuple-element.29.ordered_t_in.refs_1_, f32[4,128,512]{2,1,0:T(8,128)} %get-tuple-element.30.nd_in, bf16[4,160,128]{2,1,0:T(8,128)(2,1)} %copy-done.12, ...), custom_call_target="tpu_custom_call" | custom-call | flops 10569646080 | bytes 36700160 | tf_op jit(solution)/shard_map/pallas_call | solution.py:743
  42.7 1.9 %collective-permute-start.4 = (bf16[448,512]{1,0:T(8,128)(2,1)}, bf16[448,512]{1,0:T(8,128)(2,1)S(1)}, u32[]{:S(2)}, u32[]{:S(2)}) collective-permute-start(bf16[448,512]{1,0:T(8,128)(2,1)} %get-tuple-element.38), channel_id=1, source_target_pairs={{1,2},{2,1},{0,3},{3,0},{5,6},{6,5},{4,7},{7,4},{9,10},{10,9},{8,1... | collective-permute-start | bytes 1376264 | tf_op jit(solution)/shard_map/ppermute | solution.py:579
  44.6 1.3 %collective-permute-start.5 = (bf16[448,512]{1,0:T(8,128)(2,1)}, bf16[448,512]{1,0:T(8,128)(2,1)S(1)}, u32[]{:S(2)}, u32[]{:S(2)}) collective-permute-start(bf16[448,512]{1,0:T(8,128)(2,1)} %get-tuple-element.39), channel_id=1, source_target_pairs={{0,1},{3,2},{4,5},{7,6},{8,9},{11,10},{12,13},{15,14},{16,17},{19,... | collective-permute-start | bytes 1376264 | tf_op jit(solution)/shard_map/ppermute | solution.py:579
  45.9 4.0 %shard_map.162 = (bf16[448,512]{1,0:T(8,128)(2,1)}, bf16[448,512]{1,0:T(8,128)(2,1)}, bf16[448,512]{1,0:T(8,128)(2,1)}) custom-call(bf16[448,1792]{1,0:T(8,128)(2,1)} %w_out_in.5, bf16[128,1792]{1,0:T(8,128)(2,1)} %w_up_in.5, bf16[576,512]{1,0:T(8,128)(2,1)} %get-tuple-element.35.inputs_in.refs_2_), custom_call_target="tpu_custom_call" | custom-call | flops 1 | bytes 1 | tf_op jit(solution)/shard_map/pallas_call | solution.py:760
  49.9 4.5 %shard_map.163 = f32[4,512]{1,0:T(4,128)} custom-call(bf16[512,576]{1,0:T(8,128)(2,1)} %get-tuple-element.40.refs_0_, bf16[704,512]{1,0:T(8,128)(2,1)} %get-tuple-element.29.ordered_t_in.refs_1_, bf16[4,160,128]{2,1,0:T(8,128)(2,1)} %get-tuple-element.41.refs_2_, s32[1,512]{1,0:T(1,128)} %bitcast.7, bf16[160,16]{1,0:T(8,128)(2,1)} %constant.20.clone.left.refs_4_, ...), custom_call_target="tpu_custom_call" | custom-call | flops 1 | bytes 1 | tf_op jit(solution)/shard_map/pallas_call | solution.py:126
  54.4 1.5 %all-to-all-done.1.refs_1_ = bf16[8,736,128]{2,1,0:T(8,128)(2,1)S(1)} async-done(((bf16[8,736,128]{2,1,0:T(8,128)(2,1)}), bf16[8,736,128]{2,1,0:T(8,128)(2,1)S(1)}, u32[]{:S(2)}, u32[]{:S(2)}) %all-to-all-start.1) | async-done | bytes 1507360 | tf_op jit(solution)/shard_map/all_to_all | solution.py:563
  55.9 2.3 %shard_map.164 = bf16[4,512,128]{2,1,0:T(8,128)(2,1)} custom-call(s32[128]{0:T(128)S(1)} %copy-done.8, bf16[8,736,128]{2,1,0:T(8,128)(2,1)S(1)} %all-to-all-done.1.refs_1_, bf16[576,512]{1,0:T(8,128)(2,1)S(1)} %copy-done.1), custom_call_target="tpu_custom_call" | custom-call | flops 1 | bytes 1 | tf_op jit(solution)/shard_map/pallas_call | solution.py:126
  58.2 3.6 %all-to-all-start.2 = ((bf16[4,512,128]{2,1,0:T(8,128)(2,1)}), bf16[4,512,128]{2,1,0:T(8,128)(2,1)S(1)}, u32[]{:S(2)}, u32[]{:S(2)}) async-start(bf16[4,512,128]{2,1,0:T(8,128)(2,1)} %shard_map.164), calls=%async_computation.2 | async-start | bytes 1048576 | tf_op jit(solution)/shard_map/all_to_all | solution.py:563
  61.8 3.6 %collective-permute-done.5 = bf16[448,512]{1,0:T(8,128)(2,1)S(1)} collective-permute-done((bf16[448,512]{1,0:T(8,128)(2,1)}, bf16[448,512]{1,0:T(8,128)(2,1)S(1)}, u32[]{:S(2)}, u32[]{:S(2)}) %collective-permute-start.5) | collective-permute-done | bytes 458784 | tf_op jit(solution)/shard_map/ppermute | solution.py:579
  65.5 0.1 add_convert_fusion.1
  65.6 2.4 %collective-permute-start.7 = (bf16[448,512]{1,0:T(8,128)(2,1)S(1)}, bf16[448,512]{1,0:T(8,128)(2,1)S(1)}, u32[]{:S(2)}, u32[]{:S(2)}) collective-permute-start(bf16[448,512]{1,0:T(8,128)(2,1)S(1)} %add_convert_fusion.1), channel_id=1, source_target_pairs={{0,1},{1,0},{2,3},{3,2},{4,5},{5,4},{6,7},{7,6},{8,9},{9,8},{10,11... | collective-permute-start | bytes 1376264 | tf_op jit(solution)/shard_map/ppermute | solution.py:579
  68.0 0.1 add_convert_fusion.2
  68.2 0.7 collective-permute-start.6
  68.9 14.8 %collective-permute-done.7 = bf16[448,512]{1,0:T(8,128)(2,1)S(1)} collective-permute-done((bf16[448,512]{1,0:T(8,128)(2,1)S(1)}, bf16[448,512]{1,0:T(8,128)(2,1)S(1)}, u32[]{:S(2)}, u32[]{:S(2)}) %collective-permute-start.7) | collective-permute-done | bytes 458784 | tf_op jit(solution)/shard_map/ppermute | solution.py:579
  83.7 1.0 %fusion = bf16[512,448]{0,1:T(8,128)(2,1)} fusion(bf16[448,512]{1,0:T(8,128)(2,1)S(1)} %collective-permute-done.7, bf16[448,512]{1,0:T(8,128)(2,1)S(1)} %copy-done.9, bf16[448,512]{1,0:T(8,128)(2,1)S(1)} %collective-permute-done.6, bf16[448,512]{1,0:T(8,128)(2,1)S(1)} %collective-permute-done.4, pred[]{:T(512)S(6)} %or.3), kind=kLoop, calls=%fused_computation.3 | loop fusion | flops 1605632 | bytes 2293761 | tf_op jit(solution)/shard_map/transpose | solution.py:814
  84.7 0.6 shard_map.165
  (35 shorter events, 0.1 us)
Async XLA Ops:
  0.6 11.4 %copy-start.4 = (bf16[16,1792]{1,0:T(8,128)(2,1)S(1)}, bf16[16,1792]{1,0:T(8,128)(2,1)}, u32[]{:S(2)}) copy-start(bf16[16,1792]{1,0:T(8,128)(2,1)} %refs_3_) | copy-start | bytes 172036
  0.6 17.0 %copy-start.13 = (s32[32]{0:T(128)S(1)}, s32[32]{0:T(128)}, u32[]{:S(2)}) copy-start(s32[32]{0:T(128)} %param.23) | copy-start | bytes 388
  0.7 17.0 %copy-start.14 = (s32[32]{0:T(128)S(1)}, s32[32]{0:T(128)}, u32[]{:S(2)}) copy-start(s32[32]{0:T(128)} %param.22) | copy-start | bytes 388
  0.7 17.2 %copy-start.7 = (s32[512]{0:T(512)S(1)}, s32[512]{0:T(512)}, u32[]{:S(2)}) copy-start(s32[512]{0:T(512)} %param.21) | copy-start | bytes 6148
  6.9 17.7 %all-to-all-start = ((bf16[8,352,128]{2,1,0:T(8,128)(2,1)}), bf16[8,352,128]{2,1,0:T(8,128)(2,1)S(1)}, u32[]{:S(2)}, u32[]{:S(2)}) async-start(bf16[8,352,128]{2,1,0:T(8,128)(2,1)} %shard_map.157), calls=%async_computation | async-start | bytes 1441792 | tf_op jit(solution)/shard_map/all_to_all | solution.py:563
  12.1 9.4 %collective-permute-start.2 = (bf16[16,1792]{1,0:T(8,128)(2,1)S(1)}, bf16[16,1792]{1,0:T(8,128)(2,1)S(1)}, u32[]{:S(2)}, u32[]{:S(2)}) collective-permute-start(bf16[16,1792]{1,0:T(8,128)(2,1)S(1)} %copy-done.4), channel_id=1, source_target_pairs={{0,1},{1,2},{2,3},{3,0},{4,5},{5,6},{6,7},{7,4},{8,9},{9,10},{10,1... | collective-permute-start | bytes 172040 | tf_op jit(solution)/shard_map/ppermute | solution.py:568
  13.7 7.8 %collective-permute-start.1 = (bf16[16,1792]{1,0:T(8,128)(2,1)S(1)}, bf16[16,1792]{1,0:T(8,128)(2,1)S(1)}, u32[]{:S(2)}, u32[]{:S(2)}) collective-permute-start(bf16[16,1792]{1,0:T(8,128)(2,1)S(1)} %copy-done.4), channel_id=1, source_target_pairs={{0,2},{1,3},{2,0},{3,1},{4,6},{5,7},{6,4},{7,5},{8,10},{9,11},{10,... | collective-permute-start | bytes 172040 | tf_op jit(solution)/shard_map/ppermute | solution.py:568
  16.3 5.2 %collective-permute-start = (bf16[16,1792]{1,0:T(8,128)(2,1)S(1)}, bf16[16,1792]{1,0:T(8,128)(2,1)S(1)}, u32[]{:S(2)}, u32[]{:S(2)}) collective-permute-start(bf16[16,1792]{1,0:T(8,128)(2,1)S(1)} %copy-done.4), channel_id=1, source_target_pairs={{0,3},{1,0},{2,1},{3,2},{4,7},{5,4},{6,5},{7,6},{8,11},{9,8},{10,9... | collective-permute-start | bytes 172040 | tf_op jit(solution)/shard_map/ppermute | solution.py:568
  18.5 3.0 %copy-start = (bf16[448,1792]{1,0:T(8,128)(2,1)S(1)}, bf16[448,1792]{1,0:T(8,128)(2,1)}, u32[]{:S(2)}) copy-start(bf16[448,1792]{1,0:T(8,128)(2,1)} %w_out_in.5) | copy-start | bytes 4816900
  18.5 3.0 %copy-start.2 = (bf16[128,1792]{1,0:T(8,128)(2,1)S(1)}, bf16[128,1792]{1,0:T(8,128)(2,1)}, u32[]{:S(2)}) copy-start(bf16[128,1792]{1,0:T(8,128)(2,1)} %w_up_in.5) | copy-start | bytes 1376260
  21.4 3.2 %copy-start.3 = (f32[160,8]{1,0:T(8,128)S(1)}, f32[160,8]{1,0:T(8,128)}, u32[]{:S(2)}) copy-start(f32[160,8]{1,0:T(8,128)} %constant.22.clone.cols.refs_6_) | copy-start | bytes 15364
  21.4 3.2 %copy-start.5 = (bf16[160,16]{1,0:T(8,128)(2,1)S(1)}, bf16[160,16]{1,0:T(8,128)(2,1)}, u32[]{:S(2)}) copy-start(bf16[160,16]{1,0:T(8,128)(2,1)} %constant.21.clone.right.refs_5_) | copy-start | bytes 15364
  21.4 3.2 %copy-start.6 = (bf16[160,16]{1,0:T(8,128)(2,1)S(1)}, bf16[160,16]{1,0:T(8,128)(2,1)}, u32[]{:S(2)}) copy-start(bf16[160,16]{1,0:T(8,128)(2,1)} %constant.20.clone.left.refs_4_) | copy-start | bytes 15364
  21.4 3.2 %copy-start.8 = (s32[128]{0:T(128)S(1)}, s32[128]{0:T(128)}, u32[]{:S(2)}) copy-start(s32[128]{0:T(128)} %refs_0_.1) | copy-start | bytes 1540
  29.2 6.4 %collective-permute-start.3 = (bf16[4,160,128]{2,1,0:T(8,128)(2,1)}, bf16[4,160,128]{2,1,0:T(8,128)(2,1)S(1)}, u32[]{:S(2)}, u32[]{:S(2)}) collective-permute-start(bf16[4,160,128]{2,1,0:T(8,128)(2,1)} %get-tuple-element.33), channel_id=1, source_target_pairs={{0,4},{4,8},{8,12},{12,16},{16,20},{20,24},{24,28},{1,5},{5,9},{9,... | collective-permute-start | bytes 491528 | tf_op jit(solution)/shard_map/ppermute | solution.py:739
  30.7 25.2 %all-to-all-start.1 = ((bf16[8,736,128]{2,1,0:T(8,128)(2,1)}), bf16[8,736,128]{2,1,0:T(8,128)(2,1)S(1)}, u32[]{:S(2)}, u32[]{:S(2)}) async-start(bf16[8,736,128]{2,1,0:T(8,128)(2,1)} %shard_map.159), calls=%async_computation.1 | async-start | bytes 3014656 | tf_op jit(solution)/shard_map/all_to_all | solution.py:563
  35.5 0.7 copy-start.12
  42.7 19.2 %collective-permute-start.4 = (bf16[448,512]{1,0:T(8,128)(2,1)}, bf16[448,512]{1,0:T(8,128)(2,1)S(1)}, u32[]{:S(2)}, u32[]{:S(2)}) collective-permute-start(bf16[448,512]{1,0:T(8,128)(2,1)} %get-tuple-element.38), channel_id=1, source_target_pairs={{1,2},{2,1},{0,3},{3,0},{5,6},{6,5},{4,7},{7,4},{9,10},{10,9},{8,1... | collective-permute-start | bytes 1376264 | tf_op jit(solution)/shard_map/ppermute | solution.py:579
  44.6 20.9 %collective-permute-start.5 = (bf16[448,512]{1,0:T(8,128)(2,1)}, bf16[448,512]{1,0:T(8,128)(2,1)S(1)}, u32[]{:S(2)}, u32[]{:S(2)}) collective-permute-start(bf16[448,512]{1,0:T(8,128)(2,1)} %get-tuple-element.39), channel_id=1, source_target_pairs={{0,1},{3,2},{4,5},{7,6},{8,9},{11,10},{12,13},{15,14},{16,17},{19,... | collective-permute-start | bytes 1376264 | tf_op jit(solution)/shard_map/ppermute | solution.py:579
  45.9 10.0 %copy-start.1 = (bf16[576,512]{1,0:T(8,128)(2,1)S(1)}, bf16[576,512]{1,0:T(8,128)(2,1)}, u32[]{:S(2)}) copy-start(bf16[576,512]{1,0:T(8,128)(2,1)} %get-tuple-element.35.inputs_in.refs_2_) | copy-start | bytes 1769476
  54.4 11.1 %copy-start.10 = (bf16[448,512]{1,0:T(8,128)(2,1)S(1)}, bf16[448,512]{1,0:T(8,128)(2,1)}, u32[]{:S(2)}) copy-start(bf16[448,512]{1,0:T(8,128)(2,1)} %get-tuple-element.45) | copy-start | bytes 1376260
  58.2 9.8 %copy-start.11 = (bf16[448,512]{1,0:T(8,128)(2,1)S(1)}, bf16[448,512]{1,0:T(8,128)(2,1)}, u32[]{:S(2)}) copy-start(bf16[448,512]{1,0:T(8,128)(2,1)} %get-tuple-element.37) | copy-start | bytes 1376260
  58.2 26.5 %all-to-all-start.2 = ((bf16[4,512,128]{2,1,0:T(8,128)(2,1)}), bf16[4,512,128]{2,1,0:T(8,128)(2,1)S(1)}, u32[]{:S(2)}, u32[]{:S(2)}) async-start(bf16[4,512,128]{2,1,0:T(8,128)(2,1)} %shard_map.164), calls=%async_computation.2 | async-start | bytes 1048576 | tf_op jit(solution)/shard_map/all_to_all | solution.py:563
  61.8 21.8 %copy-start.9 = (bf16[448,512]{1,0:T(8,128)(2,1)S(1)}, bf16[448,512]{1,0:T(8,128)(2,1)}, u32[]{:S(2)}) copy-start(bf16[448,512]{1,0:T(8,128)(2,1)} %get-tuple-element.36) | copy-start | bytes 1376260
  65.6 18.0 %collective-permute-start.7 = (bf16[448,512]{1,0:T(8,128)(2,1)S(1)}, bf16[448,512]{1,0:T(8,128)(2,1)S(1)}, u32[]{:S(2)}, u32[]{:S(2)}) collective-permute-start(bf16[448,512]{1,0:T(8,128)(2,1)S(1)} %add_convert_fusion.1), channel_id=1, source_target_pairs={{0,1},{1,0},{2,3},{3,2},{4,5},{5,4},{6,7},{7,6},{8,9},{9,8},{10,11... | collective-permute-start | bytes 1376264 | tf_op jit(solution)/shard_map/ppermute | solution.py:579
  68.2 15.5 %collective-permute-start.6 = (bf16[448,512]{1,0:T(8,128)(2,1)S(1)}, bf16[448,512]{1,0:T(8,128)(2,1)S(1)}, u32[]{:S(2)}, u32[]{:S(2)}) collective-permute-start(bf16[448,512]{1,0:T(8,128)(2,1)S(1)} %add_convert_fusion.2), channel_id=1, source_target_pairs={{1,2},{2,1},{5,6},{6,5},{9,10},{10,9},{13,14},{14,13},{17,18},{18,... | collective-permute-start | bytes 1376264 | tf_op jit(solution)/shard_map/ppermute | solution.py:579

commit v2 on v1

--- a/solution.py
+++ b/solution.py
@@ -198,8 +198,8 @@
         lax.fori_loop(k * part // step, (k + 1) * part // step, norm_rows, 0, unroll=2)
     for load in weights:
         load.wait()
-    wide[:, :low] = dot(normed[...], wd[...])
-    wide[:, low:] = dot(normed[...], wq[...], ((1,), (1,)))
+    wide[:, :low] = dot(normed[...], wd[...]).astype(wide.dtype)
+    wide[:, low:] = dot(normed[...], wq[...], ((1,), (1,))).astype(wide.dtype)
     sends = []
     for g in range(groups):
         pack(picked_rows(wide, picked, g, per_peer, page_len), out.at[g], 0)
@@ -465,7 +465,7 @@
         fetches[2 * h + 1].wait()
         cross = dot(state[h], phi_of(queries[h], left, right, cols).astype(BF), ((0,), (0,)))
         both = nd[h] + carried * cross
-        inputs[h * HD : (h + 1) * HD, :] = (both[:HD, :] / both[ONE : ONE + 1, :]).astype(BF)
+        inputs[h * HD : (h + 1) * HD, :] = (both[:HD, :] * (1.0 / both[ONE : ONE + 1, :])).astype(BF)
     compute()
     kept = [start(inputs, inputs_in, sems.at[next(sem)]), start(state, state_in, sems.at[next(sem)])]
     finish()
@@ -569,11 +569,12 @@
     return [*steps, values]
 
 
+def joined(*parts):
+    return sum(part.astype(F32) for part in parts).astype(BF)
+
+
 def line_sums(far_terms, near_terms, axis, beside):
     size = lax.axis_size(axis)
-
-    def joined(*parts):
-        return sum(part.astype(F32) for part in parts).astype(BF)
 
     def send(values, *pairs):
         return lax.ppermute(values, axis, pairs)
@@ -588,7 +589,7 @@
         relayed = jnp.where(middle, across, 0)
         paired = send(joined(near_terms[1], relayed), (0, 1), (1, 0), (2, 3), (3, 2))
         centre = send(joined(near_terms[2], inward), (1, 2), (2, 1))
-        return joined(own_term, jnp.where(middle, centre, across), paired), beside
+        return (own_term, jnp.where(middle, centre, across), paired), beside
     terms = {1: near_terms[1], -1: near_terms[2], size - 1: far_terms[0], 1 - size: far_terms[0]}
     for distance in range(size - 2, 1, -1):
         terms[distance], terms[-distance] = far_terms[2 * (size - 1 - distance) - 1 :][:2]
@@ -601,7 +602,7 @@
             to_down = joined(to_down, going_down)
         going_up = send(to_up, *[(i, i + 1) for i in range(step)])
         going_down = send(to_down, *[(i, i - 1) for i in range(size - step, size)])
-    return joined(own_term, going_up, going_down), beside
+    return (own_term, going_up, going_down), beside
 
 
 def on_device(
@@ -655,7 +656,7 @@
             pltpu.VMEM((qkv_cols, model_width), BF),
             pltpu.VMEM((model_width, low), BF),
             pltpu.VMEM((count, model_width), BF),
-            pltpu.VMEM((count, sent), F32),
+            pltpu.VMEM((count, sent), F32 if page_len % 16 else BF),
             pltpu.VMEM((groups, packed, LANES), BF),
             picked,
             dma((7 + groups,)),
@@ -799,7 +800,7 @@
         1,
         1,
     )
-    update, [state_norms, _] = line_sums(far_terms, near_terms, "mp", [state_norms, logits])
+    (own_term, *others), [state_norms, _] = line_sums(far_terms, near_terms, "mp", [state_norms, logits])
     logits = exchange(logits, "mp")
     best = kernel_call(
         functools.partial(best_kernel, shards),
@@ -811,7 +812,8 @@
         1,
         32 * MIB,
     )(logits)
-    return update.T, state_norms, best.reshape(-1)
+    own_term, best = lax.optimization_barrier((own_term, best))
+    return joined(own_term, *others).T, state_norms, best.reshape(-1)
 
 
 def solution(mesh):

time: 86.7 us -> 86.2 us (level)
  waiting for transfers between devices: 19.9 us -> 18.6 us
    ppermute x4, waiting for transfers between devices: 18.4 us -> 9.39 us  [send(): return lax.ppermute(values, axis, pairs)]
    all_to_all x3, waiting for transfers between devices: 1.46 us -> 9.21 us  [exchange(): return lax.all_to_all(blocks, axis, split_axis=0, concat_axis=0, tiled=True)]
  transfers between devices with their start and end apart: 11 -> 11, of which waited for: 3 -> 4; matrix products, arithmetic and copies ran while one was open for 2% -> 1% of each run, Pallas kernels for 27% -> 28%
where the time goes in v2:
time: 86.2 us; the launch traced here: 84.7 us
  Pallas kernels  34.6 us (40%)
  starting transfers between devices  26.9 us (31%)
  waiting for transfers between devices  18.6 us (22%)
  other arithmetic  2.11 us (2%)
  local copies, waits for them, and re-layouts  1.51 us (2%)
  between operations  0.95 us (1%)
    all_to_all x3, starting transfers between devices, exchange(): return lax.all_to_all(blocks, axis, split_axis=0, concat_axis=0, tiled=True)  13.5 us
    ppermute x4, waiting for transfers between devices, send(): return lax.ppermute(values, axis, pairs)  9.39 us
    all_to_all x3, waiting for transfers between devices, exchange(): return lax.all_to_all(blocks, axis, split_axis=0, concat_axis=0, tiled=True)  9.21 us
    pallas_call x2, Pallas kernels, staged_call(): kernel_call(run, [pltpu.HBM(x.shape, x.dtype) for x in out_shape], [SMEM]...  6.84 us
    pallas_call x1, Pallas kernels, on_device(): kernel_call(functools.partial(finish_kernel, low, heads, shards), [part]...  6.47 us
    ppermute x4, starting transfers between devices, send(): return lax.ppermute(values, axis, pairs)  6.34 us
    pallas_call x1, Pallas kernels, on_device(): kernel_call(functools.partial(project_kernel, dims), pltpu.HBM((groups, p...  6.19 us
    ppermute x3, starting transfers between devices, ring_rows(): lax.ppermute(values, axis, [(i, (i + by) % size) for i in range(size)])  5.57 us
  transfers between devices with their start and end apart: 11, of which 4 were waited for; matrix products, arithmetic and copies ran while one was open for 1% of the time, Pallas kernels for 28%

profile of v2, /device:TPU:0, one launch (start us, length us, event | category | flops | bytes accessed | tf_op | source)
XLA Modules:
  0.0 84.7 jit_solution(16952379869432568188)
XLA Ops:
  0.7 6.2 %shard_map.157 = bf16[8,352,128]{2,1,0:T(8,128)(2,1)} custom-call(s32[128]{0:T(128)} %refs_0_.1, bf16[512,1792]{1,0:T(8,128)(2,1)} %hidden_in.2, f32[1792]{0:T(1024)} %gain.1, bf16[576,1792]{1,0:T(8,128)(2,1)} %bitcast.9, bf16[1792,128]{1,0:T(8,128)(2,1)} %wd_in.1), custom_call_target="tpu_custom_call" | custom-call | flops 1291845632 | bytes 4358144 | tf_op jit(solution)/shard_map/pallas_call | solution.py:649
  6.9 5.2 %all-to-all-start = ((bf16[8,352,128]{2,1,0:T(8,128)(2,1)}), bf16[8,352,128]{2,1,0:T(8,128)(2,1)S(1)}, u32[]{:S(2)}, u32[]{:S(2)}) async-start(bf16[8,352,128]{2,1,0:T(8,128)(2,1)} %shard_map.157), calls=%async_computation | async-start | bytes 1441792 | tf_op jit(solution)/shard_map/all_to_all | solution.py:563
  12.1 1.6 %collective-permute-start.2 = (bf16[16,1792]{1,0:T(8,128)(2,1)S(1)}, bf16[16,1792]{1,0:T(8,128)(2,1)S(1)}, u32[]{:S(2)}, u32[]{:S(2)}) collective-permute-start(bf16[16,1792]{1,0:T(8,128)(2,1)S(1)} %copy-done.4), channel_id=1, source_target_pairs={{0,1},{1,2},{2,3},{3,0},{4,5},{5,6},{6,7},{7,4},{8,9},{9,10},{10,1... | collective-permute-start | bytes 172040 | tf_op jit(solution)/shard_map/ppermute | solution.py:568
  13.7 2.6 %collective-permute-start.1 = (bf16[16,1792]{1,0:T(8,128)(2,1)S(1)}, bf16[16,1792]{1,0:T(8,128)(2,1)S(1)}, u32[]{:S(2)}, u32[]{:S(2)}) collective-permute-start(bf16[16,1792]{1,0:T(8,128)(2,1)S(1)} %copy-done.4), channel_id=1, source_target_pairs={{0,2},{1,3},{2,0},{3,1},{4,6},{5,7},{6,4},{7,5},{8,10},{9,11},{10,... | collective-permute-start | bytes 172040 | tf_op jit(solution)/shard_map/ppermute | solution.py:568
  16.3 1.4 %collective-permute-start = (bf16[16,1792]{1,0:T(8,128)(2,1)S(1)}, bf16[16,1792]{1,0:T(8,128)(2,1)S(1)}, u32[]{:S(2)}, u32[]{:S(2)}) collective-permute-start(bf16[16,1792]{1,0:T(8,128)(2,1)S(1)} %copy-done.4), channel_id=1, source_target_pairs={{0,3},{1,0},{2,1},{3,2},{4,7},{5,4},{6,5},{7,6},{8,11},{9,8},{10,9... | collective-permute-start | bytes 172040 | tf_op jit(solution)/shard_map/ppermute | solution.py:568
  17.6 0.2 select_reduce_fusion.1
  17.8 0.1 select_reduce_fusion
  17.9 0.6 broadcast_subtract_fusion
  18.5 2.9 %shard_map.158.refs_4_ = bf16[8,736,128]{2,1,0:T(8,128)(2,1)} custom-call(s32[128]{0:T(128)} %refs_0_.1, bf16[512,1792]{1,0:T(8,128)(2,1)} %hidden_in.2), custom_call_target="tpu_custom_call" | custom-call | flops 1 | bytes 1 | tf_op jit(solution)/shard_map/pallas_call | solution.py:678
  21.5 3.1 %shard_map.159 = bf16[8,736,128]{2,1,0:T(8,128)(2,1)} custom-call(bf16[448,1792]{1,0:T(8,128)(2,1)S(1)} %copy-done, bf16[128,1792]{1,0:T(8,128)(2,1)S(1)} %copy-done.2, bf16[16,1792]{1,0:T(8,128)(2,1)S(1)} %collective-permute-done.refs_0_, bf16[16,1792]{1,0:T(8,128)(2,1)S(1)} %collective-permute-done.1.refs_1_, ...), custom_call_target="tpu_custom_call", output_to_operand_aliasing={{}: (6, {})} | custom-call | flops 132120576 | bytes 1835008 | tf_op jit(solution)/shard_map/pallas_call | solution.py:693
  24.7 4.5 %shard_map.160 = (bf16[512,576]{1,0:T(8,128)(2,1)}, bf16[704,512]{1,0:T(8,128)(2,1)}, bf16[4,160,128]{2,1,0:T(8,128)(2,1)}, f32[4,128,512]{2,1,0:T(8,128)}) custom-call(s32[128]{0:T(128)S(1)} %copy-done.8, bf16[8,352,128]{2,1,0:T(8,128)(2,1)S(1)} %all-to-all-done.arrived, s32[1,512]{1,0:T(1,128)S(1)} %bitcast.8, bf16[160,16]{1,0:T(8,128)(2,1)S(1)} %copy-done.6, ...), custom_call_target="tpu_custom_call" | custom-call | flops 1073741824 | bytes 2162688 | tf_op jit(solution)/shard_map/pallas_call | solution.py:713
  29.2 1.5 %collective-permute-start.3 = (bf16[4,160,128]{2,1,0:T(8,128)(2,1)}, bf16[4,160,128]{2,1,0:T(8,128)(2,1)S(1)}, u32[]{:S(2)}, u32[]{:S(2)}) collective-permute-start(bf16[4,160,128]{2,1,0:T(8,128)(2,1)} %get-tuple-element.35), channel_id=1, source_target_pairs={{0,4},{4,8},{8,12},{12,16},{16,20},{20,24},{24,28},{1,5},{5,9},{9,... | collective-permute-start | bytes 491528 | tf_op jit(solution)/shard_map/ppermute | solution.py:740
  30.7 4.8 %all-to-all-start.1 = ((bf16[8,736,128]{2,1,0:T(8,128)(2,1)}), bf16[8,736,128]{2,1,0:T(8,128)(2,1)S(1)}, u32[]{:S(2)}, u32[]{:S(2)}) async-start(bf16[8,736,128]{2,1,0:T(8,128)(2,1)} %shard_map.159), calls=%async_computation.1 | async-start | bytes 3014656 | tf_op jit(solution)/shard_map/all_to_all | solution.py:563
  35.5 0.7 copy-done.14
  36.2 6.5 %shard_map.161 = (bf16[448,512]{1,0:T(8,128)(2,1)}, bf16[448,512]{1,0:T(8,128)(2,1)}, bf16[576,512]{1,0:T(8,128)(2,1)}, bf16[4,160,128]{2,1,0:T(8,128)(2,1)}) custom-call(bf16[704,512]{1,0:T(8,128)(2,1)} %get-tuple-element.31.ordered_t_in.refs_1_, f32[4,128,512]{2,1,0:T(8,128)} %get-tuple-element.32.nd_in, bf16[4,160,128]{2,1,0:T(8,128)(2,1)} %copy-done.14, ...), custom_call_target="tpu_custom_call" | custom-call | flops 10569646080 | bytes 36700160 | tf_op jit(solution)/shard_map/pallas_call | solution.py:744
  42.7 1.9 %collective-permute-start.4 = (bf16[448,512]{1,0:T(8,128)(2,1)}, bf16[448,512]{1,0:T(8,128)(2,1)S(1)}, u32[]{:S(2)}, u32[]{:S(2)}) collective-permute-start(bf16[448,512]{1,0:T(8,128)(2,1)} %get-tuple-element.42), channel_id=1, source_target_pairs={{1,2},{2,1},{0,3},{3,0},{5,6},{6,5},{4,7},{7,4},{9,10},{10,9},{8,1... | collective-permute-start | bytes 1376264 | tf_op jit(solution)/shard_map/ppermute | solution.py:580
  44.6 1.3 %collective-permute-start.5 = (bf16[448,512]{1,0:T(8,128)(2,1)}, bf16[448,512]{1,0:T(8,128)(2,1)S(1)}, u32[]{:S(2)}, u32[]{:S(2)}) collective-permute-start(bf16[448,512]{1,0:T(8,128)(2,1)} %get-tuple-element.43), channel_id=1, source_target_pairs={{0,1},{3,2},{4,5},{7,6},{8,9},{11,10},{12,13},{15,14},{16,17},{19,... | collective-permute-start | bytes 1376264 | tf_op jit(solution)/shard_map/ppermute | solution.py:580
  45.9 4.0 %shard_map.162 = (bf16[448,512]{1,0:T(8,128)(2,1)}, bf16[448,512]{1,0:T(8,128)(2,1)}, bf16[448,512]{1,0:T(8,128)(2,1)}) custom-call(bf16[448,1792]{1,0:T(8,128)(2,1)} %w_out_in.5, bf16[128,1792]{1,0:T(8,128)(2,1)} %w_up_in.5, bf16[576,512]{1,0:T(8,128)(2,1)} %get-tuple-element.37.inputs_in.refs_2_), custom_call_target="tpu_custom_call" | custom-call | flops 1 | bytes 1 | tf_op jit(solution)/shard_map/pallas_call | solution.py:761
  49.9 4.5 %shard_map.165 = f32[4,512]{1,0:T(4,128)} custom-call(bf16[512,576]{1,0:T(8,128)(2,1)} %get-tuple-element.44.refs_0_, bf16[704,512]{1,0:T(8,128)(2,1)} %get-tuple-element.31.ordered_t_in.refs_1_, bf16[4,160,128]{2,1,0:T(8,128)(2,1)} %get-tuple-element.45.refs_2_, s32[1,512]{1,0:T(1,128)} %bitcast.7, bf16[160,16]{1,0:T(8,128)(2,1)} %constant.20.clone.left.refs_4_, ...), custom_call_target="tpu_custom_call" | custom-call | flops 1 | bytes 1 | tf_op jit(solution)/shard_map/pallas_call | solution.py:126
  54.4 1.4 %all-to-all-done.1.refs_1_ = bf16[8,736,128]{2,1,0:T(8,128)(2,1)S(1)} async-done(((bf16[8,736,128]{2,1,0:T(8,128)(2,1)}), bf16[8,736,128]{2,1,0:T(8,128)(2,1)S(1)}, u32[]{:S(2)}, u32[]{:S(2)}) %all-to-all-start.1) | async-done | bytes 1507360 | tf_op jit(solution)/shard_map/all_to_all | solution.py:563
  55.9 2.3 %shard_map.163 = bf16[4,512,128]{2,1,0:T(8,128)(2,1)} custom-call(s32[128]{0:T(128)S(1)} %copy-done.8, bf16[8,736,128]{2,1,0:T(8,128)(2,1)S(1)} %all-to-all-done.1.refs_1_, bf16[576,512]{1,0:T(8,128)(2,1)S(1)} %copy-done.1), custom_call_target="tpu_custom_call" | custom-call | flops 1 | bytes 1 | tf_op jit(solution)/shard_map/pallas_call | solution.py:126
  58.2 3.5 %all-to-all-start.2 = ((bf16[4,512,128]{2,1,0:T(8,128)(2,1)}), bf16[4,512,128]{2,1,0:T(8,128)(2,1)S(1)}, u32[]{:S(2)}, u32[]{:S(2)}) async-start(bf16[4,512,128]{2,1,0:T(8,128)(2,1)} %shard_map.163), calls=%async_computation.2 | async-start | bytes 1048576 | tf_op jit(solution)/shard_map/all_to_all | solution.py:563
  61.7 3.8 %collective-permute-done.5 = bf16[448,512]{1,0:T(8,128)(2,1)S(1)} collective-permute-done((bf16[448,512]{1,0:T(8,128)(2,1)}, bf16[448,512]{1,0:T(8,128)(2,1)S(1)}, u32[]{:S(2)}, u32[]{:S(2)}) %collective-permute-start.5) | collective-permute-done | bytes 458784 | tf_op jit(solution)/shard_map/ppermute | solution.py:580
  65.5 0.8 copy-done.11
  66.2 0.1 add_convert_fusion.1
  66.4 2.4 %collective-permute-start.7 = (bf16[448,512]{1,0:T(8,128)(2,1)S(1)}, bf16[448,512]{1,0:T(8,128)(2,1)S(1)}, u32[]{:S(2)}, u32[]{:S(2)}) collective-permute-start(bf16[448,512]{1,0:T(8,128)(2,1)S(1)} %add_convert_fusion.1), channel_id=1, source_target_pairs={{0,1},{1,0},{2,3},{3,2},{4,5},{5,4},{6,7},{7,6},{8,9},{9,8},{10,11... | collective-permute-start | bytes 1376264 | tf_op jit(solution)/shard_map/ppermute | solution.py:580
  68.8 0.1 add_convert_fusion.2
  69.0 0.7 collective-permute-start.6
  69.7 7.8 %all-to-all-done.2.pieces = bf16[4,512,128]{2,1,0:T(8,128)(2,1)S(1)} async-done(((bf16[4,512,128]{2,1,0:T(8,128)(2,1)}), bf16[4,512,128]{2,1,0:T(8,128)(2,1)S(1)}, u32[]{:S(2)}, u32[]{:S(2)}) %all-to-all-start.2) | async-done | bytes 524320 | tf_op jit(solution)/shard_map/all_to_all | solution.py:563
  77.4 0.6 shard_map.164
  78.0 5.6 %collective-permute-done.7 = bf16[448,512]{1,0:T(8,128)(2,1)S(1)} collective-permute-done((bf16[448,512]{1,0:T(8,128)(2,1)S(1)}, bf16[448,512]{1,0:T(8,128)(2,1)S(1)}, u32[]{:S(2)}, u32[]{:S(2)}) %collective-permute-start.7) | collective-permute-done | bytes 458784 | tf_op jit(solution)/shard_map/ppermute | solution.py:580
  83.7 1.0 %fusion = bf16[512,448]{0,1:T(8,128)(2,1)} fusion(bf16[448,512]{1,0:T(8,128)(2,1)S(1)} %collective-permute-done.7, bf16[448,512]{1,0:T(8,128)(2,1)S(1)} %copy-done.9, bf16[448,512]{1,0:T(8,128)(2,1)S(1)} %collective-permute-done.6, bf16[448,512]{1,0:T(8,128)(2,1)S(1)} %collective-permute-done.4, pred[]{:T(512)S(6)} %or.3), kind=kLoop, calls=%fused_computation.3 | loop fusion | flops 1605632 | bytes 2293761 | tf_op jit(solution)/shard_map/transpose | solution.py:816
  (39 shorter events, 0.1 us)
Async XLA Ops:
  0.6 11.4 %copy-start.4 = (bf16[16,1792]{1,0:T(8,128)(2,1)S(1)}, bf16[16,1792]{1,0:T(8,128)(2,1)}, u32[]{:S(2)}) copy-start(bf16[16,1792]{1,0:T(8,128)(2,1)} %refs_3_) | copy-start | bytes 172036
  0.6 17.0 %copy-start.15 = (s32[32]{0:T(128)S(1)}, s32[32]{0:T(128)}, u32[]{:S(2)}) copy-start(s32[32]{0:T(128)} %param.23) | copy-start | bytes 388
  0.7 17.0 %copy-start.16 = (s32[32]{0:T(128)S(1)}, s32[32]{0:T(128)}, u32[]{:S(2)}) copy-start(s32[32]{0:T(128)} %param.22) | copy-start | bytes 388
  0.7 17.2 %copy-start.7 = (s32[512]{0:T(512)S(1)}, s32[512]{0:T(512)}, u32[]{:S(2)}) copy-start(s32[512]{0:T(512)} %param.21) | copy-start | bytes 6148
  6.9 17.7 %all-to-all-start = ((bf16[8,352,128]{2,1,0:T(8,128)(2,1)}), bf16[8,352,128]{2,1,0:T(8,128)(2,1)S(1)}, u32[]{:S(2)}, u32[]{:S(2)}) async-start(bf16[8,352,128]{2,1,0:T(8,128)(2,1)} %shard_map.157), calls=%async_computation | async-start | bytes 1441792 | tf_op jit(solution)/shard_map/all_to_all | solution.py:563
  12.1 9.4 %collective-permute-start.2 = (bf16[16,1792]{1,0:T(8,128)(2,1)S(1)}, bf16[16,1792]{1,0:T(8,128)(2,1)S(1)}, u32[]{:S(2)}, u32[]{:S(2)}) collective-permute-start(bf16[16,1792]{1,0:T(8,128)(2,1)S(1)} %copy-done.4), channel_id=1, source_target_pairs={{0,1},{1,2},{2,3},{3,0},{4,5},{5,6},{6,7},{7,4},{8,9},{9,10},{10,1... | collective-permute-start | bytes 172040 | tf_op jit(solution)/shard_map/ppermute | solution.py:568
  13.7 7.8 %collective-permute-start.1 = (bf16[16,1792]{1,0:T(8,128)(2,1)S(1)}, bf16[16,1792]{1,0:T(8,128)(2,1)S(1)}, u32[]{:S(2)}, u32[]{:S(2)}) collective-permute-start(bf16[16,1792]{1,0:T(8,128)(2,1)S(1)} %copy-done.4), channel_id=1, source_target_pairs={{0,2},{1,3},{2,0},{3,1},{4,6},{5,7},{6,4},{7,5},{8,10},{9,11},{10,... | collective-permute-start | bytes 172040 | tf_op jit(solution)/shard_map/ppermute | solution.py:568
  16.3 5.2 %collective-permute-start = (bf16[16,1792]{1,0:T(8,128)(2,1)S(1)}, bf16[16,1792]{1,0:T(8,128)(2,1)S(1)}, u32[]{:S(2)}, u32[]{:S(2)}) collective-permute-start(bf16[16,1792]{1,0:T(8,128)(2,1)S(1)} %copy-done.4), channel_id=1, source_target_pairs={{0,3},{1,0},{2,1},{3,2},{4,7},{5,4},{6,5},{7,6},{8,11},{9,8},{10,9... | collective-permute-start | bytes 172040 | tf_op jit(solution)/shard_map/ppermute | solution.py:568
  18.5 3.0 %copy-start = (bf16[448,1792]{1,0:T(8,128)(2,1)S(1)}, bf16[448,1792]{1,0:T(8,128)(2,1)}, u32[]{:S(2)}) copy-start(bf16[448,1792]{1,0:T(8,128)(2,1)} %w_out_in.5) | copy-start | bytes 4816900
  18.5 3.0 %copy-start.2 = (bf16[128,1792]{1,0:T(8,128)(2,1)S(1)}, bf16[128,1792]{1,0:T(8,128)(2,1)}, u32[]{:S(2)}) copy-start(bf16[128,1792]{1,0:T(8,128)(2,1)} %w_up_in.5) | copy-start | bytes 1376260
  21.4 3.2 %copy-start.3 = (f32[160,8]{1,0:T(8,128)S(1)}, f32[160,8]{1,0:T(8,128)}, u32[]{:S(2)}) copy-start(f32[160,8]{1,0:T(8,128)} %constant.22.clone.cols.refs_6_) | copy-start | bytes 15364
  21.4 3.2 %copy-start.5 = (bf16[160,16]{1,0:T(8,128)(2,1)S(1)}, bf16[160,16]{1,0:T(8,128)(2,1)}, u32[]{:S(2)}) copy-start(bf16[160,16]{1,0:T(8,128)(2,1)} %constant.21.clone.right.refs_5_) | copy-start | bytes 15364
  21.4 3.2 %copy-start.6 = (bf16[160,16]{1,0:T(8,128)(2,1)S(1)}, bf16[160,16]{1,0:T(8,128)(2,1)}, u32[]{:S(2)}) copy-start(bf16[160,16]{1,0:T(8,128)(2,1)} %constant.20.clone.left.refs_4_) | copy-start | bytes 15364
  21.5 3.2 %copy-start.8 = (s32[128]{0:T(128)S(1)}, s32[128]{0:T(128)}, u32[]{:S(2)}) copy-start(s32[128]{0:T(128)} %refs_0_.1) | copy-start | bytes 1540
  29.2 6.4 %collective-permute-start.3 = (bf16[4,160,128]{2,1,0:T(8,128)(2,1)}, bf16[4,160,128]{2,1,0:T(8,128)(2,1)S(1)}, u32[]{:S(2)}, u32[]{:S(2)}) collective-permute-start(bf16[4,160,128]{2,1,0:T(8,128)(2,1)} %get-tuple-element.35), channel_id=1, source_target_pairs={{0,4},{4,8},{8,12},{12,16},{16,20},{20,24},{24,28},{1,5},{5,9},{9,... | collective-permute-start | bytes 491528 | tf_op jit(solution)/shard_map/ppermute | solution.py:740
  30.7 25.2 %all-to-all-start.1 = ((bf16[8,736,128]{2,1,0:T(8,128)(2,1)}), bf16[8,736,128]{2,1,0:T(8,128)(2,1)S(1)}, u32[]{:S(2)}, u32[]{:S(2)}) async-start(bf16[8,736,128]{2,1,0:T(8,128)(2,1)} %shard_map.159), calls=%async_computation.1 | async-start | bytes 3014656 | tf_op jit(solution)/shard_map/all_to_all | solution.py:563
  35.5 0.7 copy-start.14
  42.7 19.0 %collective-permute-start.4 = (bf16[448,512]{1,0:T(8,128)(2,1)}, bf16[448,512]{1,0:T(8,128)(2,1)S(1)}, u32[]{:S(2)}, u32[]{:S(2)}) collective-permute-start(bf16[448,512]{1,0:T(8,128)(2,1)} %get-tuple-element.42), channel_id=1, source_target_pairs={{1,2},{2,1},{0,3},{3,0},{5,6},{6,5},{4,7},{7,4},{9,10},{10,9},{8,1... | collective-permute-start | bytes 1376264 | tf_op jit(solution)/shard_map/ppermute | solution.py:580
  44.6 20.9 %collective-permute-start.5 = (bf16[448,512]{1,0:T(8,128)(2,1)}, bf16[448,512]{1,0:T(8,128)(2,1)S(1)}, u32[]{:S(2)}, u32[]{:S(2)}) collective-permute-start(bf16[448,512]{1,0:T(8,128)(2,1)} %get-tuple-element.43), channel_id=1, source_target_pairs={{0,1},{3,2},{4,5},{7,6},{8,9},{11,10},{12,13},{15,14},{16,17},{19,... | collective-permute-start | bytes 1376264 | tf_op jit(solution)/shard_map/ppermute | solution.py:580
  45.9 9.9 %copy-start.1 = (bf16[576,512]{1,0:T(8,128)(2,1)S(1)}, bf16[576,512]{1,0:T(8,128)(2,1)}, u32[]{:S(2)}) copy-start(bf16[576,512]{1,0:T(8,128)(2,1)} %get-tuple-element.37.inputs_in.refs_2_) | copy-start | bytes 1769476
  54.4 11.8 %copy-start.10 = (bf16[448,512]{1,0:T(8,128)(2,1)S(1)}, bf16[448,512]{1,0:T(8,128)(2,1)}, u32[]{:S(2)}) copy-start(bf16[448,512]{1,0:T(8,128)(2,1)} %get-tuple-element.48) | copy-start | bytes 1376260
  58.2 19.2 %all-to-all-start.2 = ((bf16[4,512,128]{2,1,0:T(8,128)(2,1)}), bf16[4,512,128]{2,1,0:T(8,128)(2,1)S(1)}, u32[]{:S(2)}, u32[]{:S(2)}) async-start(bf16[4,512,128]{2,1,0:T(8,128)(2,1)} %shard_map.163), calls=%async_computation.2 | async-start | bytes 1048576 | tf_op jit(solution)/shard_map/all_to_all | solution.py:563
  61.7 7.1 %copy-start.13 = (bf16[448,512]{1,0:T(8,128)(2,1)S(1)}, bf16[448,512]{1,0:T(8,128)(2,1)}, u32[]{:S(2)}) copy-start(bf16[448,512]{1,0:T(8,128)(2,1)} %get-tuple-element.41) | copy-start | bytes 1376260
  65.5 0.8 copy-start.11
  66.2 2.6 %copy-start.12 = (bf16[448,512]{1,0:T(8,128)(2,1)S(1)}, bf16[448,512]{1,0:T(8,128)(2,1)}, u32[]{:S(2)}) copy-start(bf16[448,512]{1,0:T(8,128)(2,1)} %copy-done.11) | copy-start | bytes 1376260
  66.2 17.4 %copy-start.9 = (bf16[448,512]{1,0:T(8,128)(2,1)S(1)}, bf16[448,512]{1,0:T(8,128)(2,1)}, u32[]{:S(2)}) copy-start(bf16[448,512]{1,0:T(8,128)(2,1)} %get-tuple-element.40) | copy-start | bytes 1376260
  66.4 17.3 %collective-permute-start.7 = (bf16[448,512]{1,0:T(8,128)(2,1)S(1)}, bf16[448,512]{1,0:T(8,128)(2,1)S(1)}, u32[]{:S(2)}, u32[]{:S(2)}) collective-permute-start(bf16[448,512]{1,0:T(8,128)(2,1)S(1)} %add_convert_fusion.1), channel_id=1, source_target_pairs={{0,1},{1,0},{2,3},{3,2},{4,5},{5,4},{6,7},{7,6},{8,9},{9,8},{10,11... | collective-permute-start | bytes 1376264 | tf_op jit(solution)/shard_map/ppermute | solution.py:580
  69.0 14.7 %collective-permute-start.6 = (bf16[448,512]{1,0:T(8,128)(2,1)S(1)}, bf16[448,512]{1,0:T(8,128)(2,1)S(1)}, u32[]{:S(2)}, u32[]{:S(2)}) collective-permute-start(bf16[448,512]{1,0:T(8,128)(2,1)S(1)} %add_convert_fusion.2), channel_id=1, source_target_pairs={{1,2},{2,1},{5,6},{6,5},{9,10},{10,9},{13,14},{14,13},{17,18},{18,... | collective-permute-start | bytes 1376264 | tf_op jit(solution)/shard_map/ppermute | solution.py:580

commit v3 on v2

--- a/solution.py
+++ b/solution.py
@@ -552,6 +552,28 @@
         norms[h : h + 1, :] = jnp.sqrt(total / (counted * float(FEAT * HD)))
 
 
+def relay_kernel(across, inward, paired_in, centre_in, to_pair_in, to_centre_in, paired, centre, sems):
+    loads = [start(paired_in, paired, sems.at[0]), start(centre_in, centre, sems.at[1])]
+    here = lax.axis_index("mp")
+    middle = (here == 1) | (here == 2)
+    for load in loads:
+        load.wait()
+
+    @pl.when(middle)
+    def _():
+        paired[...] = (paired[...].astype(F32) + across[...].astype(F32)).astype(BF)
+
+    sends = [start(paired, to_pair_in, sems.at[2])]
+
+    @pl.when(middle)
+    def _():
+        centre[...] = (centre[...].astype(F32) + inward[...].astype(F32)).astype(BF)
+
+    sends.append(start(centre, to_centre_in, sems.at[3]))
+    for copy in sends:
+        copy.wait()
+
+
 def best_kernel(shards, pieces, best):
     whole = pieces[0].astype(F32)
     for i in range(1, shards):
@@ -586,9 +608,19 @@
         across = send(far_terms[0], (1, 2), (2, 1), (0, 3), (3, 0))
         inward = send(far_terms[1], (0, 1), (3, 2))
         across, inward, beside = lax.optimization_barrier((across, inward, beside))
-        relayed = jnp.where(middle, across, 0)
-        paired = send(joined(near_terms[1], relayed), (0, 1), (1, 0), (2, 3), (3, 2))
-        centre = send(joined(near_terms[2], inward), (1, 2), (2, 1))
+        whole = own_term.shape
+        to_pair, to_centre = kernel_call(
+            relay_kernel,
+            [pltpu.HBM(whole, BF)] * 2,
+            [VMEM, VMEM, ANY, ANY],
+            [ANY, ANY],
+            [pltpu.VMEM(whole, BF), pltpu.VMEM(whole, BF), pltpu.SemaphoreType.DMA((4,))],
+            1,
+            1,
+            VMEM_LIMIT - 416 * 1024,
+        )(across, inward, near_terms[1], near_terms[2])
+        paired = send(to_pair, (0, 1), (1, 0), (2, 3), (3, 2))
+        centre = send(to_centre, (1, 2), (2, 1))
         return (own_term, jnp.where(middle, centre, across), paired), beside
     terms = {1: near_terms[1], -1: near_terms[2], size - 1: far_terms[0], 1 - size: far_terms[0]}
     for distance in range(size - 2, 1, -1):

time: 86.2 us -> 103 us (1.19)
  the two profiles are of different devices: /device:TPU:0 before, /device:TPU:2 now
where the time goes in v3:
time: 103 us; the launch traced here: 102 us
  Pallas kernels  37.8 us (37%)
  waiting for transfers between devices  29.7 us (29%)
  starting transfers between devices  28.4 us (28%)
  other arithmetic  2.87 us (3%)
  local copies, waits for them, and re-layouts  2.56 us (2%)
    ppermute x1, waiting for transfers between devices, on_device(): lax.ppermute(state, 'group', [(i, i + 1) for i in range(groups - 1)])  17.5 us
    all_to_all x3, starting transfers between devices, exchange(): return lax.all_to_all(blocks, axis, split_axis=0, concat_axis=0, tiled=True)  12.1 us
    ppermute x4, waiting for transfers between devices, send(): return lax.ppermute(values, axis, pairs)  11.5 us
    ppermute x4, starting transfers between devices, send(): return lax.ppermute(values, axis, pairs)  8.75 us
    pallas_call x2, Pallas kernels, staged_call(): kernel_call(run, [pltpu.HBM(x.shape, x.dtype) for x in out_shape], [SMEM]...  6.83 us
    pallas_call x1, Pallas kernels, on_device(): kernel_call(functools.partial(finish_kernel, low, heads, shards), [part]...  6.47 us
    pallas_call x1, Pallas kernels, on_device(): kernel_call(functools.partial(project_kernel, dims), pltpu.HBM((groups, p...  6.19 us
    ppermute x3, starting transfers between devices, ring_rows(): lax.ppermute(values, axis, [(i, (i + by) % size) for i in range(size)])  5.52 us
  transfers between devices with their start and end apart: 11, of which 4 were waited for; matrix products, arithmetic and copies ran while one was open for 1% of the time, Pallas kernels for 26%

profile of v3, /device:TPU:2, one launch (start us, length us, event | category | flops | bytes accessed | tf_op | source)
XLA Modules:
  0.0 102.2 jit_solution(6054152291562071295)
XLA Ops:
  0.7 6.2 %shard_map.157 = bf16[8,352,128]{2,1,0:T(8,128)(2,1)} custom-call(s32[128]{0:T(128)} %refs_0_.1, bf16[512,1792]{1,0:T(8,128)(2,1)} %hidden_in.2, f32[1792]{0:T(1024)} %gain.1, bf16[576,1792]{1,0:T(8,128)(2,1)} %bitcast.9, bf16[1792,128]{1,0:T(8,128)(2,1)} %wd_in.1), custom_call_target="tpu_custom_call" | custom-call | flops 1291845632 | bytes 4358144 | tf_op jit(solution)/shard_map/pallas_call | solution.py:681
  6.9 4.3 %all-to-all-start = ((bf16[8,352,128]{2,1,0:T(8,128)(2,1)}), bf16[8,352,128]{2,1,0:T(8,128)(2,1)S(1)}, u32[]{:S(2)}, u32[]{:S(2)}) async-start(bf16[8,352,128]{2,1,0:T(8,128)(2,1)} %shard_map.157), calls=%async_computation | async-start | bytes 1441792 | tf_op jit(solution)/shard_map/all_to_all | solution.py:585
  11.1 1.6 %collective-permute-start.2 = (bf16[16,1792]{1,0:T(8,128)(2,1)S(1)}, bf16[16,1792]{1,0:T(8,128)(2,1)S(1)}, u32[]{:S(2)}, u32[]{:S(2)}) collective-permute-start(bf16[16,1792]{1,0:T(8,128)(2,1)S(1)} %copy-done.4), channel_id=1, source_target_pairs={{0,1},{1,2},{2,3},{3,0},{4,5},{5,6},{6,7},{7,4},{8,9},{9,10},{10,1... | collective-permute-start | bytes 172040 | tf_op jit(solution)/shard_map/ppermute | solution.py:590
  12.7 2.6 %collective-permute-start.1 = (bf16[16,1792]{1,0:T(8,128)(2,1)S(1)}, bf16[16,1792]{1,0:T(8,128)(2,1)S(1)}, u32[]{:S(2)}, u32[]{:S(2)}) collective-permute-start(bf16[16,1792]{1,0:T(8,128)(2,1)S(1)} %copy-done.4), channel_id=1, source_target_pairs={{0,2},{1,3},{2,0},{3,1},{4,6},{5,7},{6,4},{7,5},{8,10},{9,11},{10,... | collective-permute-start | bytes 172040 | tf_op jit(solution)/shard_map/ppermute | solution.py:590
  15.3 1.4 %collective-permute-start = (bf16[16,1792]{1,0:T(8,128)(2,1)S(1)}, bf16[16,1792]{1,0:T(8,128)(2,1)S(1)}, u32[]{:S(2)}, u32[]{:S(2)}) collective-permute-start(bf16[16,1792]{1,0:T(8,128)(2,1)S(1)} %copy-done.4), channel_id=1, source_target_pairs={{0,3},{1,0},{2,1},{3,2},{4,7},{5,4},{6,5},{7,6},{8,11},{9,8},{10,9... | collective-permute-start | bytes 172040 | tf_op jit(solution)/shard_map/ppermute | solution.py:590
  16.7 0.2 select_reduce_fusion.1
  16.8 0.1 select_reduce_fusion
  16.9 0.6 broadcast_subtract_fusion
  17.5 2.9 %shard_map.158.refs_4_ = bf16[8,736,128]{2,1,0:T(8,128)(2,1)} custom-call(s32[128]{0:T(128)} %refs_0_.1, bf16[512,1792]{1,0:T(8,128)(2,1)} %hidden_in.2), custom_call_target="tpu_custom_call" | custom-call | flops 1 | bytes 1 | tf_op jit(solution)/shard_map/pallas_call | solution.py:710
  20.5 3.1 %shard_map.159 = bf16[8,736,128]{2,1,0:T(8,128)(2,1)} custom-call(bf16[448,1792]{1,0:T(8,128)(2,1)S(1)} %copy-done, bf16[128,1792]{1,0:T(8,128)(2,1)S(1)} %copy-done.2, bf16[16,1792]{1,0:T(8,128)(2,1)S(1)} %collective-permute-done.refs_0_, bf16[16,1792]{1,0:T(8,128)(2,1)S(1)} %collective-permute-done.1.refs_1_, ...), custom_call_target="tpu_custom_call", output_to_operand_aliasing={{}: (6, {})} | custom-call | flops 132120576 | bytes 1835008 | tf_op jit(solution)/shard_map/pallas_call | solution.py:725
  23.7 4.5 %shard_map.160 = (bf16[512,576]{1,0:T(8,128)(2,1)}, bf16[704,512]{1,0:T(8,128)(2,1)}, bf16[4,160,128]{2,1,0:T(8,128)(2,1)}, f32[4,128,512]{2,1,0:T(8,128)}) custom-call(s32[128]{0:T(128)S(1)} %copy-done.8, bf16[8,352,128]{2,1,0:T(8,128)(2,1)S(1)} %all-to-all-done.arrived, s32[1,512]{1,0:T(1,128)S(1)} %bitcast.8, bf16[160,16]{1,0:T(8,128)(2,1)S(1)} %copy-done.6, ...), custom_call_target="tpu_custom_call" | custom-call | flops 1073741824 | bytes 2162688 | tf_op jit(solution)/shard_map/pallas_call | solution.py:745
  28.2 4.3 %all-to-all-start.1 = ((bf16[8,736,128]{2,1,0:T(8,128)(2,1)}), bf16[8,736,128]{2,1,0:T(8,128)(2,1)S(1)}, u32[]{:S(2)}, u32[]{:S(2)}) async-start(bf16[8,736,128]{2,1,0:T(8,128)(2,1)} %shard_map.159), calls=%async_computation.1 | async-start | bytes 3014656 | tf_op jit(solution)/shard_map/all_to_all | solution.py:585
  32.6 2.0 %collective-permute-start.3 = (bf16[4,160,128]{2,1,0:T(8,128)(2,1)S(1)}, bf16[4,160,128]{2,1,0:T(8,128)(2,1)S(1)}, u32[]{:S(2)}, u32[]{:S(2)}) collective-permute-start(bf16[4,160,128]{2,1,0:T(8,128)(2,1)S(1)} %copy-done.12), channel_id=1, source_target_pairs={{0,4},{4,8},{8,12},{12,16},{16,20},{20,24},{24,28},{1,5},{5,9},{9,... | collective-permute-start | bytes 491528 | tf_op jit(solution)/shard_map/ppermute | solution.py:772
  34.6 17.5 %collective-permute-done.3.state = bf16[4,160,128]{2,1,0:T(8,128)(2,1)S(1)} collective-permute-done((bf16[4,160,128]{2,1,0:T(8,128)(2,1)S(1)}, bf16[4,160,128]{2,1,0:T(8,128)(2,1)S(1)}, u32[]{:S(2)}, u32[]{:S(2)}) %collective-permute-start.3) | collective-permute-done | bytes 163872 | tf_op jit(solution)/shard_map/ppermute | solution.py:772
  52.1 0.7 copy-done.13
  52.8 6.5 %shard_map.161 = (bf16[448,512]{1,0:T(8,128)(2,1)}, bf16[448,512]{1,0:T(8,128)(2,1)}, bf16[576,512]{1,0:T(8,128)(2,1)}, bf16[4,160,128]{2,1,0:T(8,128)(2,1)}) custom-call(bf16[704,512]{1,0:T(8,128)(2,1)} %get-tuple-element.33.ordered_t_in.refs_1_, f32[4,128,512]{2,1,0:T(8,128)} %get-tuple-element.34.nd_in, bf16[4,160,128]{2,1,0:T(8,128)(2,1)} %copy-done.13, ...), custom_call_target="tpu_custom_call" | custom-call | flops 10569646080 | bytes 36700160 | tf_op jit(solution)/shard_map/pallas_call | solution.py:776
  59.3 2.1 %collective-permute-start.4 = (bf16[448,512]{1,0:T(8,128)(2,1)}, bf16[448,512]{1,0:T(8,128)(2,1)S(1)}, u32[]{:S(2)}, u32[]{:S(2)}) collective-permute-start(bf16[448,512]{1,0:T(8,128)(2,1)} %get-tuple-element.43), channel_id=1, source_target_pairs={{1,2},{2,1},{0,3},{3,0},{5,6},{6,5},{4,7},{7,4},{9,10},{10,9},{8,1... | collective-permute-start | bytes 1376264 | tf_op jit(solution)/shard_map/ppermute | solution.py:602
  61.4 1.3 %collective-permute-start.5 = (bf16[448,512]{1,0:T(8,128)(2,1)}, bf16[448,512]{1,0:T(8,128)(2,1)S(1)}, u32[]{:S(2)}, u32[]{:S(2)}) collective-permute-start(bf16[448,512]{1,0:T(8,128)(2,1)} %get-tuple-element.44), channel_id=1, source_target_pairs={{0,1},{3,2},{4,5},{7,6},{8,9},{11,10},{12,13},{15,14},{16,17},{19,... | collective-permute-start | bytes 1376264 | tf_op jit(solution)/shard_map/ppermute | solution.py:602
  62.7 1.1 %copy-done.1 = bf16[576,512]{1,0:T(8,128)(2,1)S(1)} copy-done((bf16[576,512]{1,0:T(8,128)(2,1)S(1)}, bf16[576,512]{1,0:T(8,128)(2,1)}, u32[]{:S(2)}) %copy-start.1) | copy-done | bytes 589848
  63.8 2.3 %shard_map.163 = bf16[4,512,128]{2,1,0:T(8,128)(2,1)} custom-call(s32[128]{0:T(128)S(1)} %copy-done.8, bf16[8,736,128]{2,1,0:T(8,128)(2,1)S(1)} %all-to-all-done.1.refs_1_, bf16[576,512]{1,0:T(8,128)(2,1)S(1)} %copy-done.1), custom_call_target="tpu_custom_call" | custom-call | flops 1 | bytes 1 | tf_op jit(solution)/shard_map/pallas_call | solution.py:126
  66.1 3.5 %all-to-all-start.2 = ((bf16[4,512,128]{2,1,0:T(8,128)(2,1)}), bf16[4,512,128]{2,1,0:T(8,128)(2,1)S(1)}, u32[]{:S(2)}, u32[]{:S(2)}) async-start(bf16[4,512,128]{2,1,0:T(8,128)(2,1)} %shard_map.163), calls=%async_computation.2 | async-start | bytes 1048576 | tf_op jit(solution)/shard_map/all_to_all | solution.py:585
  69.6 3.9 %shard_map.162 = (bf16[448,512]{1,0:T(8,128)(2,1)}, bf16[448,512]{1,0:T(8,128)(2,1)}, bf16[448,512]{1,0:T(8,128)(2,1)}) custom-call(bf16[448,1792]{1,0:T(8,128)(2,1)} %w_out_in.5, bf16[128,1792]{1,0:T(8,128)(2,1)} %w_up_in.5, bf16[576,512]{1,0:T(8,128)(2,1)} %get-tuple-element.39.inputs_in.refs_2_), custom_call_target="tpu_custom_call" | custom-call | flops 1 | bytes 1 | tf_op jit(solution)/shard_map/pallas_call | solution.py:793
  73.5 4.5 %shard_map.165 = f32[4,512]{1,0:T(4,128)} custom-call(bf16[512,576]{1,0:T(8,128)(2,1)} %get-tuple-element.45.refs_0_, bf16[704,512]{1,0:T(8,128)(2,1)} %get-tuple-element.33.ordered_t_in.refs_1_, bf16[4,160,128]{2,1,0:T(8,128)(2,1)} %get-tuple-element.46.refs_2_, s32[1,512]{1,0:T(1,128)} %bitcast.7, bf16[160,16]{1,0:T(8,128)(2,1)} %constant.18.clone.left.refs_4_, ...), custom_call_target="tpu_custom_call" | custom-call | flops 1 | bytes 1 | tf_op jit(solution)/shard_map/pallas_call | solution.py:126
  78.1 4.5 %collective-permute-done.5.inward = bf16[448,512]{1,0:T(8,128)(2,1)S(1)} collective-permute-done((bf16[448,512]{1,0:T(8,128)(2,1)}, bf16[448,512]{1,0:T(8,128)(2,1)S(1)}, u32[]{:S(2)}, u32[]{:S(2)}) %collective-permute-start.5) | collective-permute-done | bytes 458784 | tf_op jit(solution)/shard_map/ppermute | solution.py:602
  82.5 0.8 copy-done.11
  83.3 3.3 %shard_map.166 = (bf16[448,512]{1,0:T(8,128)(2,1)}, bf16[448,512]{1,0:T(8,128)(2,1)}) custom-call(bf16[448,512]{1,0:T(8,128)(2,1)} %copy-done.9, bf16[448,512]{1,0:T(8,128)(2,1)} %copy-done.11, bf16[448,512]{1,0:T(8,128)(2,1)} %get-tuple-element.49.paired_in, bf16[448,512]{1,0:T(8,128)(2,1)} %get-tuple-element.50.centre_in), custom_call_target="tpu_custom_call" | custom-call | flops 1 | bytes 1 | tf_op jit(solution)/shard_map/pallas_call | solution.py:612
  86.6 0.7 collective-permute-start.6
  87.3 4.6 %collective-permute-start.7 = (bf16[448,512]{1,0:T(8,128)(2,1)}, bf16[448,512]{1,0:T(8,128)(2,1)S(1)}, u32[]{:S(2)}, u32[]{:S(2)}) collective-permute-start(bf16[448,512]{1,0:T(8,128)(2,1)} %get-tuple-element.52), channel_id=1, source_target_pairs={{0,1},{1,0},{2,3},{3,2},{4,5},{5,4},{6,7},{7,6},{8,9},{9,8},{10,11... | collective-permute-start | bytes 1376264 | tf_op jit(solution)/shard_map/ppermute | solution.py:602
  91.9 0.6 all-to-all-done.2.pieces
  92.5 0.6 shard_map.164
  93.1 7.1 %collective-permute-done.7 = bf16[448,512]{1,0:T(8,128)(2,1)S(1)} collective-permute-done((bf16[448,512]{1,0:T(8,128)(2,1)}, bf16[448,512]{1,0:T(8,128)(2,1)S(1)}, u32[]{:S(2)}, u32[]{:S(2)}) %collective-permute-start.7) | collective-permute-done | bytes 458784 | tf_op jit(solution)/shard_map/ppermute | solution.py:602
  100.2 2.0 %fusion = bf16[512,448]{0,1:T(8,128)(2,1)} fusion(bf16[448,512]{1,0:T(8,128)(2,1)S(1)} %collective-permute-done.7, bf16[448,512]{1,0:T(8,128)(2,1)S(1)} %copy-done.10, bf16[448,512]{1,0:T(8,128)(2,1)S(1)} %collective-permute-done.6, bf16[448,512]{1,0:T(8,128)(2,1)} %copy-done.9, pred[]{:T(512)S(6)} %or.3), kind=kLoop, calls=%fused_computation.1 | loop fusion | flops 1605632 | bytes 2293761 | tf_op jit(solution)/shard_map/transpose | solution.py:848
  (36 shorter events, 0.1 us)
Async XLA Ops:
  0.6 10.5 %copy-start.4 = (bf16[16,1792]{1,0:T(8,128)(2,1)S(1)}, bf16[16,1792]{1,0:T(8,128)(2,1)}, u32[]{:S(2)}) copy-start(bf16[16,1792]{1,0:T(8,128)(2,1)} %refs_3_) | copy-start | bytes 172036
  0.6 16.0 %copy-start.14 = (s32[32]{0:T(128)S(1)}, s32[32]{0:T(128)}, u32[]{:S(2)}) copy-start(s32[32]{0:T(128)} %param.23) | copy-start | bytes 388
  0.7 16.0 %copy-start.15 = (s32[32]{0:T(128)S(1)}, s32[32]{0:T(128)}, u32[]{:S(2)}) copy-start(s32[32]{0:T(128)} %param.22) | copy-start | bytes 388
  0.7 16.2 %copy-start.7 = (s32[512]{0:T(512)S(1)}, s32[512]{0:T(512)}, u32[]{:S(2)}) copy-start(s32[512]{0:T(512)} %param.21) | copy-start | bytes 6148
  6.9 16.8 %all-to-all-start = ((bf16[8,352,128]{2,1,0:T(8,128)(2,1)}), bf16[8,352,128]{2,1,0:T(8,128)(2,1)S(1)}, u32[]{:S(2)}, u32[]{:S(2)}) async-start(bf16[8,352,128]{2,1,0:T(8,128)(2,1)} %shard_map.157), calls=%async_computation | async-start | bytes 1441792 | tf_op jit(solution)/shard_map/all_to_all | solution.py:585
  11.1 9.4 %collective-permute-start.2 = (bf16[16,1792]{1,0:T(8,128)(2,1)S(1)}, bf16[16,1792]{1,0:T(8,128)(2,1)S(1)}, u32[]{:S(2)}, u32[]{:S(2)}) collective-permute-start(bf16[16,1792]{1,0:T(8,128)(2,1)S(1)} %copy-done.4), channel_id=1, source_target_pairs={{0,1},{1,2},{2,3},{3,0},{4,5},{5,6},{6,7},{7,4},{8,9},{9,10},{10,1... | collective-permute-start | bytes 172040 | tf_op jit(solution)/shard_map/ppermute | solution.py:590
  12.7 7.8 %collective-permute-start.1 = (bf16[16,1792]{1,0:T(8,128)(2,1)S(1)}, bf16[16,1792]{1,0:T(8,128)(2,1)S(1)}, u32[]{:S(2)}, u32[]{:S(2)}) collective-permute-start(bf16[16,1792]{1,0:T(8,128)(2,1)S(1)} %copy-done.4), channel_id=1, source_target_pairs={{0,2},{1,3},{2,0},{3,1},{4,6},{5,7},{6,4},{7,5},{8,10},{9,11},{10,... | collective-permute-start | bytes 172040 | tf_op jit(solution)/shard_map/ppermute | solution.py:590
  15.3 5.2 %collective-permute-start = (bf16[16,1792]{1,0:T(8,128)(2,1)S(1)}, bf16[16,1792]{1,0:T(8,128)(2,1)S(1)}, u32[]{:S(2)}, u32[]{:S(2)}) collective-permute-start(bf16[16,1792]{1,0:T(8,128)(2,1)S(1)} %copy-done.4), channel_id=1, source_target_pairs={{0,3},{1,0},{2,1},{3,2},{4,7},{5,4},{6,5},{7,6},{8,11},{9,8},{10,9... | collective-permute-start | bytes 172040 | tf_op jit(solution)/shard_map/ppermute | solution.py:590
  17.5 3.0 %copy-start = (bf16[448,1792]{1,0:T(8,128)(2,1)S(1)}, bf16[448,1792]{1,0:T(8,128)(2,1)}, u32[]{:S(2)}) copy-start(bf16[448,1792]{1,0:T(8,128)(2,1)} %w_out_in.5) | copy-start | bytes 4816900
  17.5 3.0 %copy-start.2 = (bf16[128,1792]{1,0:T(8,128)(2,1)S(1)}, bf16[128,1792]{1,0:T(8,128)(2,1)}, u32[]{:S(2)}) copy-start(bf16[128,1792]{1,0:T(8,128)(2,1)} %w_up_in.5) | copy-start | bytes 1376260
  20.4 3.2 %copy-start.3 = (f32[160,8]{1,0:T(8,128)S(1)}, f32[160,8]{1,0:T(8,128)}, u32[]{:S(2)}) copy-start(f32[160,8]{1,0:T(8,128)} %constant.20.clone.cols.refs_6_) | copy-start | bytes 15364
  20.5 3.2 %copy-start.5 = (bf16[160,16]{1,0:T(8,128)(2,1)S(1)}, bf16[160,16]{1,0:T(8,128)(2,1)}, u32[]{:S(2)}) copy-start(bf16[160,16]{1,0:T(8,128)(2,1)} %constant.19.clone.right.refs_5_) | copy-start | bytes 15364
  20.5 3.2 %copy-start.6 = (bf16[160,16]{1,0:T(8,128)(2,1)S(1)}, bf16[160,16]{1,0:T(8,128)(2,1)}, u32[]{:S(2)}) copy-start(bf16[160,16]{1,0:T(8,128)(2,1)} %constant.18.clone.left.refs_4_) | copy-start | bytes 15364
  20.5 3.2 %copy-start.8 = (s32[128]{0:T(128)S(1)}, s32[128]{0:T(128)}, u32[]{:S(2)}) copy-start(s32[128]{0:T(128)} %refs_0_.1) | copy-start | bytes 1540
  28.2 4.4 %copy-start.12 = (bf16[4,160,128]{2,1,0:T(8,128)(2,1)S(1)}, bf16[4,160,128]{2,1,0:T(8,128)(2,1)}, u32[]{:S(2)}) copy-start(bf16[4,160,128]{2,1,0:T(8,128)(2,1)} %get-tuple-element.37) | copy-start | bytes 491524
  28.2 34.5 %all-to-all-start.1 = ((bf16[8,736,128]{2,1,0:T(8,128)(2,1)}), bf16[8,736,128]{2,1,0:T(8,128)(2,1)S(1)}, u32[]{:S(2)}, u32[]{:S(2)}) async-start(bf16[8,736,128]{2,1,0:T(8,128)(2,1)} %shard_map.159), calls=%async_computation.1 | async-start | bytes 3014656 | tf_op jit(solution)/shard_map/all_to_all | solution.py:585
  32.6 19.6 %collective-permute-start.3 = (bf16[4,160,128]{2,1,0:T(8,128)(2,1)S(1)}, bf16[4,160,128]{2,1,0:T(8,128)(2,1)S(1)}, u32[]{:S(2)}, u32[]{:S(2)}) collective-permute-start(bf16[4,160,128]{2,1,0:T(8,128)(2,1)S(1)} %copy-done.12), channel_id=1, source_target_pairs={{0,4},{4,8},{8,12},{12,16},{16,20},{20,24},{24,28},{1,5},{5,9},{9,... | collective-permute-start | bytes 491528 | tf_op jit(solution)/shard_map/ppermute | solution.py:772
  52.1 0.7 copy-start.13
  59.3 18.8 %collective-permute-start.4 = (bf16[448,512]{1,0:T(8,128)(2,1)}, bf16[448,512]{1,0:T(8,128)(2,1)S(1)}, u32[]{:S(2)}, u32[]{:S(2)}) collective-permute-start(bf16[448,512]{1,0:T(8,128)(2,1)} %get-tuple-element.43), channel_id=1, source_target_pairs={{1,2},{2,1},{0,3},{3,0},{5,6},{6,5},{4,7},{7,4},{9,10},{10,9},{8,1... | collective-permute-start | bytes 1376264 | tf_op jit(solution)/shard_map/ppermute | solution.py:602
  61.4 21.1 %collective-permute-start.5 = (bf16[448,512]{1,0:T(8,128)(2,1)}, bf16[448,512]{1,0:T(8,128)(2,1)S(1)}, u32[]{:S(2)}, u32[]{:S(2)}) collective-permute-start(bf16[448,512]{1,0:T(8,128)(2,1)} %get-tuple-element.44), channel_id=1, source_target_pairs={{0,1},{3,2},{4,5},{7,6},{8,9},{11,10},{12,13},{15,14},{16,17},{19,... | collective-permute-start | bytes 1376264 | tf_op jit(solution)/shard_map/ppermute | solution.py:602
  62.7 1.1 %copy-start.1 = (bf16[576,512]{1,0:T(8,128)(2,1)S(1)}, bf16[576,512]{1,0:T(8,128)(2,1)}, u32[]{:S(2)}) copy-start(bf16[576,512]{1,0:T(8,128)(2,1)} %get-tuple-element.39.inputs_in.refs_2_) | copy-start | bytes 1769476
  66.1 26.4 %all-to-all-start.2 = ((bf16[4,512,128]{2,1,0:T(8,128)(2,1)}), bf16[4,512,128]{2,1,0:T(8,128)(2,1)S(1)}, u32[]{:S(2)}, u32[]{:S(2)}) async-start(bf16[4,512,128]{2,1,0:T(8,128)(2,1)} %shard_map.163), calls=%async_computation.2 | async-start | bytes 1048576 | tf_op jit(solution)/shard_map/all_to_all | solution.py:585
  78.0 22.2 %copy-start.10 = (bf16[448,512]{1,0:T(8,128)(2,1)S(1)}, bf16[448,512]{1,0:T(8,128)(2,1)}, u32[]{:S(2)}) copy-start(bf16[448,512]{1,0:T(8,128)(2,1)} %get-tuple-element.42) | copy-start | bytes 1376260
  78.0 4.5 %copy-start.9 = (bf16[448,512]{1,0:T(8,128)(2,1)}, bf16[448,512]{1,0:T(8,128)(2,1)S(1)}, u32[]{:S(2)}) copy-start(bf16[448,512]{1,0:T(8,128)(2,1)S(1)} %collective-permute-done.4.across) | copy-start | bytes 1376260
  82.5 0.8 copy-start.11
  86.6 6.5 %collective-permute-start.6 = (bf16[448,512]{1,0:T(8,128)(2,1)}, bf16[448,512]{1,0:T(8,128)(2,1)S(1)}, u32[]{:S(2)}, u32[]{:S(2)}) collective-permute-start(bf16[448,512]{1,0:T(8,128)(2,1)} %get-tuple-element.51), channel_id=1, source_target_pairs={{1,2},{2,1},{5,6},{6,5},{9,10},{10,9},{13,14},{14,13},{17,18},{18,... | collective-permute-start | bytes 1376264 | tf_op jit(solution)/shard_map/ppermute | solution.py:602
  87.3 12.9 %collective-permute-start.7 = (bf16[448,512]{1,0:T(8,128)(2,1)}, bf16[448,512]{1,0:T(8,128)(2,1)S(1)}, u32[]{:S(2)}, u32[]{:S(2)}) collective-permute-start(bf16[448,512]{1,0:T(8,128)(2,1)} %get-tuple-element.52), channel_id=1, source_target_pairs={{0,1},{1,0},{2,3},{3,2},{4,5},{5,4},{6,7},{7,6},{8,9},{9,8},{10,11... | collective-permute-start | bytes 1376264 | tf_op jit(solution)/shard_map/ppermute | solution.py:602
